TPU v7x, 32 devices: a whole 2x2x4 slice. The times are simulated.
32 devices in a mesh: samp: 8 (over y, x, core), tok: 4 (over z).
Axes of the slice: x: 2, y: 2, z: 4, core: 2. Of those that a mesh axis runs over, the one named last changes fastest.
Arguments:
- tokens_in: bfloat16 [16, 768, 768], P('samp', 'tok'), may hold values from -6 to 6
- cotangent: float32 [16, 768, 768], P('samp', 'tok'), may hold values from -6 to 6
- singles: bfloat16 [1, 768, 384], P(None, 'tok'), may hold values from -6 to 6
- noise_table: float32 [256, 384], replicated, may hold values from -6 to 6
- noise_level: int32 [16], P('samp'), may hold values from 0 to 255
- pad_mask: int32 [1, 768], replicated, may hold values from 0 to 1, as said below
- pairwise: bfloat16 [1, 768, 768, 128], P(None, 'tok', 'samp'), may hold values from -6 to 6
- conditioner: bfloat16 [384, 4608], P(None, ('samp', 'tok')), may hold values from -0.3125 to 0.3125
- offsets: bfloat16 [3072], P(('samp', 'tok')), may hold values from -5 to 5
- shifts: bfloat16 [1536], P(('samp', 'tok')), may hold values from -5 to 5
- projector: bfloat16 [768, 3072], P(('samp', 'tok')), may hold values from -0.21875 to 0.21875
- querybias: bfloat16 [768], P(('samp', 'tok')), may hold values from -3 to 3
- combiner: bfloat16 [768, 768], P(('samp', 'tok')), may hold values from -4 to 4
- expander: bfloat16 [768, 3072], P(('samp', 'tok')), may hold values from -0.21875 to 0.21875
- reducer: bfloat16 [1536, 768], P(('samp', 'tok')), may hold values from -0.15625 to 0.15625
- pairhead: bfloat16 [128, 16], replicated, may hold values from -0.5 to 0.5
Outputs:
- mixed: bfloat16 [16, 768, 768], P('samp', 'tok')
- tokens_grad: float32 [16, 768, 768], P('samp', 'tok')
- singles_grad: float32 [1, 768, 384], P(None, 'tok', 'samp')
- pairwise_grad: float32 [1, 768, 768, 128], P(None, 'tok', 'samp')
- noise_grad: float32 [256, 384], replicated
- conditioner_grad: float32 [384, 4608], P(None, ('samp', 'tok'))
- offsets_grad: float32 [3072], P(('samp', 'tok'))
- shifts_grad: float32 [1536], P(('samp', 'tok'))
- projector_grad: float32 [768, 3072], P(('samp', 'tok'))
- querybias_grad: float32 [768], P(('samp', 'tok'))
- combiner_grad: float32 [768, 768], P(('samp', 'tok'))
- expander_grad: float32 [768, 3072], P(('samp', 'tok'))
- reducer_grad: float32 [1536, 768], P(('samp', 'tok'))
- pairhead_grad: float32 [128, 16], replicated
Inputs may be any that keep to these rules, and one draw needn't show every extreme that they name: `pad_mask`: in each structure token 0 is real and at least one token is padding; padding may stand anywhere.
All inputs are finite; a program needn't handle non-finite values.
Results may differ from a plain program's by a relative error of at most 0.015.
The roundings to bfloat16 on the way count: a program that leaves them out, or rounds other values in their place, can miss the bound.
Values may be sent and summed in bfloat16 or wider, within the bound.
No kernel may reach another device: no remote copies, remote signals or barrier semaphores. Data moves between devices by JAX's collectives and lax.ppermute only.
A program may use at most 192 MiB of HBM per device.

v0:
```python
import jax
import jax.numpy as jnp
from jax import lax
from jax.sharding import PartitionSpec as P

D = 768
H = 16
FF = 1536
N = 768
S_DEV = 2
STRUCTS = 1
LEVELS = 256
KEYB = 256
DH = 48


epsilon = 1e-05
highest = lax.Precision.HIGHEST
blocked = 1000000000.0


def normalized_tokens(values):
    center = values - jnp.mean(values, axis=-1, keepdims=True)
    inverse = lax.rsqrt(jnp.mean(center * center, axis=-1, keepdims=True) + epsilon)
    return (center * inverse, inverse)


def norm_back(normal, inverse, upstream):
    first_mean = jnp.mean(upstream, axis=-1, keepdims=True)
    second_mean = jnp.mean(upstream * normal, axis=-1, keepdims=True)
    return inverse * (upstream - first_mean - normal * second_mean)


def sigmoid_slope(sigma):
    return sigma * (1.0 - sigma)


def full_offsets(offsets, shifts):
    scale_parts = jnp.split(offsets, 4)
    shift_parts = jnp.split(shifts, 2)
    return jnp.concatenate(
        [
            scale_parts[0],
            shift_parts[0],
            scale_parts[1],
            scale_parts[2],
            shift_parts[1],
            scale_parts[3],
        ]
    )


def owner_split(gradient, position, samp_count, tok_count):
    shape = gradient.shape
    length = shape[position]
    return gradient.reshape(
        shape[:position]
        + (samp_count, tok_count, length // (samp_count * tok_count))
        + shape[position + 1 :]
    )


def owner_merge(gradient, position):
    shape = gradient.shape
    return gradient.reshape(
        shape[:position]
        + (shape[position] * shape[position + 1] * shape[position + 2],)
        + shape[position + 3 :]
    )


def per_device(
    tokens_in,
    cotangent,
    singles,
    noise_table,
    noise_level,
    pad_mask,
    pairwise,
    conditioner,
    offsets,
    shifts,
    projector,
    querybias,
    combiner,
    expander,
    reducer,
    pairhead,
):
    local_rows = tokens_in.shape[1]
    columns = pairwise.shape[2]
    dot_scale = DH ** (-0.5)
    blocks_count = N // KEYB
    sample_ids = lax.axis_index("samp") * S_DEV + jnp.arange(S_DEV, dtype=jnp.int32)
    structure = sample_ids % STRUCTS
    chooser = (structure[:, None] == jnp.arange(STRUCTS, dtype=jnp.int32)[None, :]).astype(
        jnp.float32
    )
    level_hot = (noise_level[:, None] == jnp.arange(LEVELS, dtype=jnp.int32)[None, :]).astype(
        jnp.float32
    )
    gathered = (
        lax.all_gather(conditioner, ("samp", "tok"), axis=1, tiled=True),
        lax.all_gather(offsets, ("samp", "tok"), axis=0, tiled=True),
        lax.all_gather(shifts, ("samp", "tok"), axis=0, tiled=True),
        lax.all_gather(projector, ("samp", "tok"), axis=0, tiled=True),
        lax.all_gather(querybias, ("samp", "tok"), axis=0, tiled=True),
        lax.all_gather(combiner, ("samp", "tok"), axis=0, tiled=True),
        lax.all_gather(expander, ("samp", "tok"), axis=0, tiled=True),
        lax.all_gather(reducer, ("samp", "tok"), axis=0, tiled=True),
    )
    (
        cond_full,
        offset_full,
        shift_full,
        proj_full,
        querybias_full,
        comb_full,
        expand_full,
        reduce_full,
    ) = gathered
    single_rows = jnp.einsum("as,sqc->aqc", chooser, singles.astype(jnp.float32), precision=highest)
    noise_rows = jnp.dot(level_hot, noise_table, precision=highest)
    cond_norm, cond_inverse = normalized_tokens(single_rows + noise_rows[:, None, :])
    cond_low = cond_norm.astype(jnp.bfloat16)
    bias_vector = full_offsets(offset_full.astype(jnp.float32), shift_full.astype(jnp.float32))
    adaptive_modulation = (
        jnp.dot(cond_low, cond_full, preferred_element_type=jnp.float32) + bias_vector
    )
    (
        before_norm_scale,
        before_norm_shift,
        before_gate_input,
        after_norm_scale,
        after_norm_shift,
        after_gate_output,
    ) = jnp.split(adaptive_modulation, 6, axis=-1)
    tokens = tokens_in.astype(jnp.float32)
    before_normalized, preinverse = normalized_tokens(tokens)
    before_norm_gain = jax.nn.sigmoid(before_norm_scale)
    before_hidden_units = (before_norm_gain * before_normalized + before_norm_shift).astype(
        jnp.bfloat16
    )
    streams = jnp.dot(before_hidden_units, proj_full, preferred_element_type=jnp.float32)
    query = (streams[..., :D] + querybias_full.astype(jnp.float32)).astype(jnp.bfloat16)
    keys_own = streams[..., D : 2 * D].astype(jnp.bfloat16)
    values_own = streams[..., 2 * D : 3 * D].astype(jnp.bfloat16)
    gating = jax.nn.sigmoid(streams[..., 3 * D :])
    pair_norm, pair_inverse = normalized_tokens(pairwise.astype(jnp.float32))
    pair_low = pair_norm.astype(jnp.bfloat16)
    bias_piece = jnp.einsum(
        "sqjc,ch->sjhq", pair_low, pairhead, preferred_element_type=jnp.float32
    ).astype(jnp.bfloat16)
    bias_all = lax.all_gather(
        bias_piece.reshape(STRUCTS, columns, H * local_rows), "samp", axis=1, tiled=True
    ).reshape(STRUCTS, N, H, local_rows)
    keys_all, values_all = (
        lax.all_gather(keys_own, "tok", axis=1, tiled=True),
        lax.all_gather(values_own, "tok", axis=1, tiled=True),
    )
    query_heads = query.reshape(S_DEV, local_rows, H, DH)
    keys_heads = keys_all.reshape(S_DEV, N, H, DH)
    values_heads = values_all.reshape(S_DEV, N, H, DH)
    mask_add = (jnp.take(pad_mask, structure, axis=0).astype(jnp.float32) - 1.0) * blocked

    def block_scores(first_key):
        keys_block = lax.dynamic_slice_in_dim(keys_heads, first_key, KEYB, 1)
        bias_block = jnp.take(
            lax.dynamic_slice_in_dim(bias_all, first_key, KEYB, 1), structure, axis=0
        )
        mask_block = lax.dynamic_slice_in_dim(mask_add, first_key, KEYB, 1)
        logits = (
            jnp.einsum(
                "akhd,aqhd->akhq", keys_block, query_heads, preferred_element_type=jnp.float32
            )
            * dot_scale
        )
        return logits + bias_block.astype(jnp.float32) + mask_block[:, :, None, None]

    def max_pass(running, block_index):
        running_max, denominator = running
        logits = block_scores(block_index * KEYB)
        new_max = jnp.maximum(running_max, jnp.max(logits, axis=1))
        denominator = denominator * jnp.exp(running_max - new_max) + jnp.sum(
            jnp.exp(logits - new_max[:, None]), axis=1
        )
        return ((new_max, denominator), None)

    stat_zeros = jnp.zeros((S_DEV, H, local_rows), jnp.float32)
    (row_max, row_total), unused = lax.scan(
        max_pass, (stat_zeros - 1e30, stat_zeros), jnp.arange(blocks_count)
    )
    log_total = row_max + jnp.log(row_total)

    def value_pass(accum, block_index):
        first_key = block_index * KEYB
        probs_low = jnp.exp(block_scores(first_key) - log_total[:, None]).astype(jnp.bfloat16)
        values_block = lax.dynamic_slice_in_dim(values_heads, first_key, KEYB, 1)
        return (
            accum
            + jnp.einsum(
                "akhq,akhd->aqhd", probs_low, values_block, preferred_element_type=jnp.float32
            ),
            None,
        )

    head_zeros = jnp.zeros((S_DEV, local_rows, H, DH), jnp.float32)
    attended_heads, unused = lax.scan(value_pass, head_zeros, jnp.arange(blocks_count))
    attended = attended_heads.reshape(S_DEV, local_rows, D)
    gated = (gating * attended).astype(jnp.bfloat16)
    branch = jnp.dot(gated, comb_full, preferred_element_type=jnp.float32)
    pregate_sig = jax.nn.sigmoid(before_gate_input)
    residual = tokens + pregate_sig * branch
    postnormal, postinverse = normalized_tokens(residual)
    postgain = jax.nn.sigmoid(after_norm_scale)
    posthidden = (postgain * postnormal + after_norm_shift).astype(jnp.bfloat16)
    upgate = jnp.dot(posthidden, expand_full, preferred_element_type=jnp.float32)
    preact = upgate[..., :FF]
    upper = upgate[..., FF:]
    preact_sig = jax.nn.sigmoid(preact)
    swished = preact * preact_sig
    activated = (swished * upper).astype(jnp.bfloat16)
    trans = jnp.dot(activated, reduce_full, preferred_element_type=jnp.float32)
    postgate_sig = jax.nn.sigmoid(after_gate_output)
    mixed = (residual + postgate_sig * trans).astype(jnp.bfloat16)
    cond_weights, proj_weights, comb_weights, expand_weights, reduce_weights = (
        lax.all_gather(conditioner, ("samp", "tok"), axis=1, tiled=True),
        lax.all_gather(projector, ("samp", "tok"), axis=0, tiled=True),
        lax.all_gather(combiner, ("samp", "tok"), axis=0, tiled=True),
        lax.all_gather(expander, ("samp", "tok"), axis=0, tiled=True),
        lax.all_gather(reducer, ("samp", "tok"), axis=0, tiled=True),
    )
    trans_back = (postgate_sig * cotangent).astype(jnp.bfloat16)
    postgate_back = cotangent * trans * sigmoid_slope(postgate_sig)
    reducer_part = jnp.einsum(
        "aqf,aqd->fd", activated, trans_back, preferred_element_type=jnp.float32
    )
    activated_back = jnp.einsum(
        "aqd,fd->aqf", trans_back, reduce_weights, preferred_element_type=jnp.float32
    )
    preact_back = activated_back * upper * preact_sig * (1.0 + preact * (1.0 - preact_sig))
    upgate_back = jnp.concatenate([preact_back, activated_back * swished], axis=-1).astype(
        jnp.bfloat16
    )
    expander_part = jnp.einsum(
        "aqd,aqf->df", posthidden, upgate_back, preferred_element_type=jnp.float32
    )
    posthidden_back = jnp.einsum(
        "aqf,df->aqd", upgate_back, expand_weights, preferred_element_type=jnp.float32
    )
    postscale_back = posthidden_back * postnormal * sigmoid_slope(postgain)
    residual_back = cotangent + norm_back(postnormal, postinverse, posthidden_back * postgain)
    branch_back = (pregate_sig * residual_back).astype(jnp.bfloat16)
    pregate_back = residual_back * branch * sigmoid_slope(pregate_sig)
    combiner_part = jnp.einsum(
        "aqe,aqd->ed", gated, branch_back, preferred_element_type=jnp.float32
    )
    gated_back = jnp.einsum(
        "aqd,ed->aqe", branch_back, comb_weights, preferred_element_type=jnp.float32
    )
    attended_back = (gating * gated_back).astype(jnp.bfloat16)
    gating_back = attended * gated_back * sigmoid_slope(gating)
    grad_heads = attended_back.reshape(S_DEV, local_rows, H, DH)

    def delta_pass(deltas, block_index):
        first_key = block_index * KEYB
        probs = jnp.exp(block_scores(first_key) - log_total[:, None])
        values_block = lax.dynamic_slice_in_dim(values_heads, first_key, KEYB, 1)
        probs_back = jnp.einsum(
            "aqhd,akhd->akhq", grad_heads, values_block, preferred_element_type=jnp.float32
        )
        return (deltas + jnp.sum(probs * probs_back, axis=1), None)

    deltas, unused = lax.scan(delta_pass, stat_zeros, jnp.arange(blocks_count))

    def grad_pass(running, block_index):
        query_back, keys_back, values_back, bias_back = running
        first_key = block_index * KEYB
        probs = jnp.exp(block_scores(first_key) - log_total[:, None])
        keys_block = lax.dynamic_slice_in_dim(keys_heads, first_key, KEYB, 1)
        values_block = lax.dynamic_slice_in_dim(values_heads, first_key, KEYB, 1)
        probs_back = jnp.einsum(
            "aqhd,akhd->akhq", grad_heads, values_block, preferred_element_type=jnp.float32
        )
        logits_back = probs * (probs_back - deltas[:, None])
        logits_low = logits_back.astype(jnp.bfloat16)
        query_back = (
            query_back
            + jnp.einsum(
                "akhq,akhd->aqhd", logits_low, keys_block, preferred_element_type=jnp.float32
            )
            * dot_scale
        )
        keys_piece = (
            jnp.einsum(
                "akhq,aqhd->akhd", logits_low, query_heads, preferred_element_type=jnp.float32
            )
            * dot_scale
        )
        values_piece = jnp.einsum(
            "akhq,aqhd->akhd",
            probs.astype(jnp.bfloat16),
            grad_heads,
            preferred_element_type=jnp.float32,
        )
        bias_block = jnp.einsum("as,akhq->skhq", chooser, logits_back, precision=highest)
        keys_back = lax.dynamic_update_slice_in_dim(keys_back, keys_piece, first_key, 1)
        values_back = lax.dynamic_update_slice_in_dim(values_back, values_piece, first_key, 1)
        bias_back = lax.dynamic_update_slice_in_dim(bias_back, bias_block, first_key, 1)
        return ((query_back, keys_back, values_back, bias_back), None)

    grad_zeros = jnp.zeros((S_DEV, N, H, DH), jnp.float32)
    bias_zeros = jnp.zeros((STRUCTS, N, H, local_rows), jnp.float32)
    (query_back, keys_back, values_back, bias_back), unused = lax.scan(
        grad_pass, (head_zeros, grad_zeros, grad_zeros, bias_zeros), jnp.arange(blocks_count)
    )
    keys_sum, values_sum = (
        lax.psum_scatter(
            keys_back.reshape(S_DEV, N, D).astype(jnp.bfloat16),
            "tok",
            scatter_dimension=1,
            tiled=True,
        ).astype(jnp.float32),
        lax.psum_scatter(
            values_back.reshape(S_DEV, N, D).astype(jnp.bfloat16),
            "tok",
            scatter_dimension=1,
            tiled=True,
        ).astype(jnp.float32),
    )
    query_flat = query_back.reshape(S_DEV, local_rows, D)
    querybias_part = jnp.sum(query_flat, axis=(0, 1))
    streams_back = jnp.concatenate([query_flat, keys_sum, values_sum, gating_back], axis=-1).astype(
        jnp.bfloat16
    )
    projector_part = jnp.einsum(
        "aqd,aqe->de", before_hidden_units, streams_back, preferred_element_type=jnp.float32
    )
    prehidden_back = jnp.einsum(
        "aqe,de->aqd", streams_back, proj_weights, preferred_element_type=jnp.float32
    )
    prescale_back = prehidden_back * before_normalized * sigmoid_slope(before_norm_gain)
    tokens_grad = residual_back + norm_back(
        before_normalized, preinverse, prehidden_back * before_norm_gain
    )
    adapt_back = jnp.concatenate(
        [
            prescale_back,
            prehidden_back,
            pregate_back,
            postscale_back,
            posthidden_back,
            postgate_back,
        ],
        axis=-1,
    )
    adapt_sums = jnp.sum(adapt_back, axis=(0, 1))
    sum_blocks = jnp.split(adapt_sums, 6)
    offsets_part = jnp.concatenate([sum_blocks[0], sum_blocks[2], sum_blocks[3], sum_blocks[5]])
    shifts_part = jnp.concatenate([sum_blocks[1], sum_blocks[4]])
    adapt_low = adapt_back.astype(jnp.bfloat16)
    conditioner_part = jnp.einsum(
        "aqc,aqe->ce", cond_low, adapt_low, preferred_element_type=jnp.float32
    )
    cond_grad = norm_back(
        cond_norm,
        cond_inverse,
        jnp.einsum("aqe,ce->aqc", adapt_low, cond_weights, preferred_element_type=jnp.float32),
    )
    singles_part = jnp.einsum("as,aqc->sqc", chooser, cond_grad, precision=highest)
    noise_part = jnp.dot(level_hot.T, jnp.sum(cond_grad, axis=1), precision=highest)
    bias_sum, singles_grad = (
        lax.psum_scatter(
            bias_back.reshape(STRUCTS, N, H * local_rows), "samp", scatter_dimension=1, tiled=True
        ),
        lax.psum_scatter(singles_part, "samp", scatter_dimension=2, tiled=True),
    )
    bias_owned = bias_sum.reshape(STRUCTS, columns, H, local_rows)
    pair_part = jnp.einsum(
        "sqjc,sjhq->ch", pair_low.astype(jnp.float32), bias_owned, precision=highest
    )
    pair_norm_back = jnp.einsum(
        "sjhq,ch->sqjc", bias_owned, pairhead.astype(jnp.float32), precision=highest
    )
    pairwise_grad = norm_back(pair_norm, pair_inverse, pair_norm_back)
    noise_grad, pairhead_grad = lax.psum((noise_part, pair_part), ("samp", "tok"))
    samp_count = lax.axis_size("samp")
    tok_count = lax.axis_size("tok")
    divided = (
        owner_split(conditioner_part, 1, samp_count, tok_count),
        owner_split(offsets_part, 0, samp_count, tok_count),
        owner_split(shifts_part, 0, samp_count, tok_count),
        owner_split(projector_part, 0, samp_count, tok_count),
        owner_split(querybias_part, 0, samp_count, tok_count),
        owner_split(combiner_part, 0, samp_count, tok_count),
        owner_split(expander_part, 0, samp_count, tok_count),
        owner_split(reducer_part, 0, samp_count, tok_count),
    )
    sectioned = (
        lax.psum_scatter(
            divided[0].astype(jnp.bfloat16), "tok", scatter_dimension=2, tiled=True
        ).astype(jnp.float32),
        lax.psum_scatter(
            divided[1].astype(jnp.bfloat16), "tok", scatter_dimension=1, tiled=True
        ).astype(jnp.float32),
        lax.psum_scatter(
            divided[2].astype(jnp.bfloat16), "tok", scatter_dimension=1, tiled=True
        ).astype(jnp.float32),
        lax.psum_scatter(
            divided[3].astype(jnp.bfloat16), "tok", scatter_dimension=1, tiled=True
        ).astype(jnp.float32),
        lax.psum_scatter(
            divided[4].astype(jnp.bfloat16), "tok", scatter_dimension=1, tiled=True
        ).astype(jnp.float32),
        lax.psum_scatter(
            divided[5].astype(jnp.bfloat16), "tok", scatter_dimension=1, tiled=True
        ).astype(jnp.float32),
        lax.psum_scatter(
            divided[6].astype(jnp.bfloat16), "tok", scatter_dimension=1, tiled=True
        ).astype(jnp.float32),
        lax.psum_scatter(
            divided[7].astype(jnp.bfloat16), "tok", scatter_dimension=1, tiled=True
        ).astype(jnp.float32),
    )
    summed = (
        lax.psum_scatter(sectioned[0], "samp", scatter_dimension=1, tiled=True),
        lax.psum_scatter(sectioned[1], "samp", scatter_dimension=0, tiled=True),
        lax.psum_scatter(sectioned[2], "samp", scatter_dimension=0, tiled=True),
        lax.psum_scatter(sectioned[3], "samp", scatter_dimension=0, tiled=True),
        lax.psum_scatter(sectioned[4], "samp", scatter_dimension=0, tiled=True),
        lax.psum_scatter(sectioned[5], "samp", scatter_dimension=0, tiled=True),
        lax.psum_scatter(sectioned[6], "samp", scatter_dimension=0, tiled=True),
        lax.psum_scatter(sectioned[7], "samp", scatter_dimension=0, tiled=True),
    )
    conditioner_grad = owner_merge(summed[0], 1)
    offsets_grad = owner_merge(summed[1], 0)
    shifts_grad = owner_merge(summed[2], 0)
    projector_grad = owner_merge(summed[3], 0)
    querybias_grad = owner_merge(summed[4], 0)
    combiner_grad = owner_merge(summed[5], 0)
    expander_grad = owner_merge(summed[6], 0)
    reducer_grad = owner_merge(summed[7], 0)
    return (
        mixed,
        tokens_grad,
        singles_grad,
        pairwise_grad,
        noise_grad,
        conditioner_grad,
        offsets_grad,
        shifts_grad,
        projector_grad,
        querybias_grad,
        combiner_grad,
        expander_grad,
        reducer_grad,
        pairhead_grad,
    )


def solution(mesh):
    in_specs = (
        P("samp", "tok", None),
        P("samp", "tok", None),
        P(None, "tok", None),
        P(),
        P("samp"),
        P(),
        P(None, "tok", "samp", None),
        P(None, ("samp", "tok")),
        P(("samp", "tok")),
        P(("samp", "tok")),
        P(("samp", "tok"), None),
        P(("samp", "tok")),
        P(("samp", "tok"), None),
        P(("samp", "tok"), None),
        P(("samp", "tok"), None),
        P(),
    )
    out_specs = (
        P("samp", "tok", None),
        P("samp", "tok", None),
        P(None, "tok", "samp"),
        P(None, "tok", "samp", None),
        P(),
        P(None, ("samp", "tok")),
        P(("samp", "tok")),
        P(("samp", "tok")),
        P(("samp", "tok"), None),
        P(("samp", "tok")),
        P(("samp", "tok"), None),
        P(("samp", "tok"), None),
        P(("samp", "tok"), None),
        P(),
    )
    return jax.shard_map(
        per_device, mesh=mesh, in_specs=in_specs, out_specs=out_specs, check_vma=False
    )
```

profile of v0, /device:TPU:0, one launch (start us, length us, event | category | flops | bytes accessed | tf_op | source)
XLA Modules:
  0.0 1893.5 jit_solution(9991954900450061131)
XLA Ops:
  8.7 5.8 convert_reduce_fusion
  14.6 8.5 fusion.67
  23.9 8.0 fusion.103
  34.4 42.6 %all-reduce.16 = (bf16[3072]{0:T(1024)(128)(2,1)S(1)}, bf16[1536]{0:T(1024)(128)(2,1)S(1)}, bf16[768]{0:T(1024)(128)(2,1)S(1)}) all-reduce(bf16[3072]{0:T(1024)(128)(2,1)S(1)} %dynamic-update-slice, bf16[1536]{0:T(1024)(128)(2,1)S(1)} %dynamic-update-slice.1, ...), channel_id=1, replica_groups=mesh['samp'=8,'tok'=4] {'samp','tok'}, use_global_device_ids=true, to_apply=%add | all-reduce | flops 5376 | bytes 21504
  85.8 53.7 %all-gather.11.cloned.1.call-done = bf16[768,3072]{1,0:T(8,128)(2,1)} async-done(((bf16[24,3072]{1,0:T(8,128)(2,1)}), bf16[768,3072]{1,0:T(8,128)(2,1)}) %all-gather.11.cloned.1.call-update) | async-done | bytes 4718608 | tf_op jit(solution)/shard_map/all_gather | solution.py:106
  139.5 6.5 fusion.200
  150.1 29.6 %all-gather.17.cloned.1.call-done = bf16[1,768,3072]{2,1,0:T(8,128)(2,1)} async-done(((bf16[1,96,3072]{2,1,0:T(8,128)(2,1)}), bf16[1,768,3072]{2,1,0:T(8,128)(2,1)}) %all-gather.17.cloned.1.call-update) | async-done | bytes 4718608 | tf_op jit(solution)/shard_map/all_gather | solution.py:154
  179.7 6.7 copy.110
  188.9 43.3 %all-gather.15.cloned.1.call-done = bf16[2,768,768]{2,1,0:T(8,128)(2,1)} async-done(((bf16[2,192,768]{2,1,0:T(8,128)(2,1)}), bf16[2,768,768]{2,1,0:T(8,128)(2,1)}) %all-gather.15.cloned.1.call-update) | async-done | bytes 2359312 | tf_op jit(solution)/shard_map/all_gather | solution.py:158
  236.5 39.1 %while.57 = (s32[]{:T(128)}, f32[2,16,192]{2,1,0:T(8,128)S(1)}, f32[2,16,192]{2,1,0:T(8,128)S(1)}, s32[3]{0:T(128)S(1)}, bf16[2,768,16,48]{1,3,2,0:T(8,128)(2,1)...) while((s32[]{:T(128)}, f32[2,16,192]{2,1,0:T(8,128)S(1)}, ...), condition=%wide.region_9.11_spmd.clone, body=%wide.region_6.0_spmd.clone.sunk | while | flops 165967872 | bytes 27656424 | solution.py:190
  239.7 5.5 fusion.253
  245.2 4.4 exponential_reduce_fusion.2
  252.7 5.4 fusion.253
  258.1 4.4 exponential_reduce_fusion.2
  265.7 5.4 fusion.253
  271.1 4.4 exponential_reduce_fusion.2
  275.6 7.4 all-gather.13.cloned.1.call-done
  285.8 34.1 %while.58 = (s32[]{:T(128)}, f32[2,192,16,48]{1,3,2,0:T(8,128)}, s32[3]{0:T(128)S(1)}, bf16[2,768,16,48]{1,3,2,0:T(8,128)(2,1)S(1)}, bf16[2,768,16,48]{1,3,2,0:T...) while((s32[]{:T(128)}, f32[2,192,16,48]{1,3,2,0:T(8,128)}, ...), condition=%wide.region_11.13_spmd.clone, body=%wide.region_10.12_spmd.clone.sunk | while | flops 311230464 | bytes 13016784 | solution.py:208
  290.5 6.2 bitcast_add_fusion.8
  301.4 6.7 bitcast_add_fusion.8
  312.8 6.7 bitcast_add_fusion.8
  326.7 11.9 all-gather.19.cloned.1.call-done
  346.3 57.6 %all-gather.21.cloned.1.call-done = bf16[768,3072]{1,0:T(8,128)(2,1)} async-done(((bf16[24,3072]{1,0:T(8,128)(2,1)}), bf16[768,3072]{1,0:T(8,128)(2,1)}) %all-gather.21.cloned.1.call-update) | async-done | bytes 4718608 | tf_op jit(solution)/shard_map/all_gather | solution.py:109
  403.9 6.7 fusion.72
  410.6 52.3 %all-gather.23.cloned.1.call-done = bf16[1536,768]{1,0:T(8,128)(2,1)} async-done(((bf16[48,768]{1,0:T(8,128)(2,1)}), bf16[1536,768]{1,0:T(8,128)(2,1)}) %all-gather.23.cloned.1.call-update) | async-done | bytes 2359312 | tf_op jit(solution)/shard_map/all_gather | solution.py:110
  462.9 6.2 multiply_convert_fusion.1
  469.1 5.4 fusion.190
  481.0 27.9 %while.59 = (s32[]{:T(128)}, f32[2,16,192]{2,1,0:T(8,128)S(1)}, s32[3]{0:T(128)S(1)}, bf16[2,768,16,48]{1,3,2,0:T(8,128)(2,1)}, bf16[2,192,16,48]{1,3,2,0:T(8,12...) while((s32[]{:T(128)}, f32[2,16,192]{2,1,0:T(8,128)S(1)}, ...), condition=%wide.region_18.20_spmd.clone, body=%wide.region_16.19_spmd.clone.sunk | while | flops 312219648 | bytes 23328992 | solution.py:274
  512.0 4.7 broadcast_in_dim.23.clone
  516.7 153.5 %while.60 = (s32[]{:T(128)}, f32[2,192,16,48]{1,3,2,0:T(8,128)}, bf16[2,768,16,48]{1,3,2,0:T(8,128)(2,1)}, bf16[2,768,16,48]{1,3,2,0:T(8,128)(2,1)}, f32[1,768,1...) while((s32[]{:T(128)}, f32[2,192,16,48]{1,3,2,0:T(8,128)}, ...), condition=%wide.region_20.22_spmd.clone, body=%wide.region_19.21_spmd.clone.sunk | while | flops 796360704 | bytes 198074976 | solution.py:314
  523.3 5.5 bitcast_multiply_fusion.3
  528.8 5.5 bitcast_add_fusion.9
  542.4 23.2 %fusion.278 = f32[1,256,16,192]{1,0,3,2:T(1,128)S(1)} fusion(f32[2,256,16,192]{1,3,2,0:T(8,128)S(1)} %copy-done.2), kind=kOutput, calls=%fused_computation.45.clone.1 | convolution fusion | flops 18874368 | bytes 9437184 | tf_op jit(solution)/shard_map/while/body/eval_jaxpr/as,akhq->skhq/dot_general | solution.py:306
  574.1 5.5 bitcast_multiply_fusion.3
  579.7 5.9 bitcast_add_fusion.9
  593.7 23.2 %fusion.278 = f32[1,256,16,192]{1,0,3,2:T(1,128)S(1)} fusion(f32[2,256,16,192]{1,3,2,0:T(8,128)S(1)} %copy-done.2), kind=kOutput, calls=%fused_computation.45.clone.1 | convolution fusion | flops 18874368 | bytes 9437184 | tf_op jit(solution)/shard_map/while/body/eval_jaxpr/as,akhq->skhq/dot_general | solution.py:306
  625.5 5.5 bitcast_multiply_fusion.3
  631.0 5.9 bitcast_add_fusion.9
  645.1 23.2 %fusion.278 = f32[1,256,16,192]{1,0,3,2:T(1,128)S(1)} fusion(f32[2,256,16,192]{1,3,2,0:T(8,128)S(1)} %copy-done.2), kind=kOutput, calls=%fused_computation.45.clone.1 | convolution fusion | flops 18874368 | bytes 9437184 | tf_op jit(solution)/shard_map/while/body/eval_jaxpr/as,akhq->skhq/dot_general | solution.py:306
  670.3 4.5 copy.114
  687.0 4.5 bitcast_convert_fusion.4
  691.4 30.5 %reduce-scatter.20.cloned.1.call-done = bf16[2,192,768]{2,1,0:T(8,128)(2,1)} async-done(((bf16[2,768,768]{2,1,0:T(8,128)(2,1)}), bf16[2,192,768]{2,1,0:T(8,128)(2,1)}) %reduce-scatter.20.cloned.1.call-update) | async-done | bytes 589840 | tf_op jit(solution)/shard_map/reduce_scatter | solution.py:324
  721.9 49.7 %reduce-scatter.18.cloned.1.call-done = bf16[2,192,768]{2,1,0:T(8,128)(2,1)} async-done(((bf16[2,768,768]{2,1,0:T(8,128)(2,1)}), bf16[2,192,768]{2,1,0:T(8,128)(2,1)}) %reduce-scatter.18.cloned.1.call-update) | async-done | bytes 589840 | tf_op jit(solution)/shard_map/reduce_scatter | solution.py:318
  771.7 5.6 fusion.189
  791.8 5.9 copy.119
  797.7 4.7 bitcast_convert_fusion.5
  802.5 20.8 %copy.118 = f32[1,768,3072]{2,0,1:T(1,128)} copy(f32[1,768,3072]{1,2,0:T(8,128)} %bitcast.307) | data formatting | bytes 18874368 | tf_op jit(solution)/shard_map/reshape | solution.py:374
  823.8 6.2 fusion.191
  834.8 524.8 %all-reduce.27.cloned.1.call-done = (bf16[384,8,4,144]{0,3,2,1:T(8,128)(2,1)}, bf16[8,4,24,3072]{3,2,1,0:T(8,128)(2,1)}, bf16[8,4,24,768]{3,2,1,0:T(8,128)(2,1)}...) async-done(((bf16[384,8,4,144]{0,3,2,1:T(8,128)(2,1)}, bf16[8,4,24,3072]{3,2,1,0:T(8,128)(2,1)}, bf16[8,4,24,768]{3,2,1,0:T(8,128)(2,1)}, ...) | async-done | bytes 16515088
  1373.4 126.8 %all-reduce.25.cloned.1.call-done = f32[1,768,3072]{2,0,1:T(1,128)} async-done(((f32[1,768,3072]{2,0,1:T(1,128)}), f32[1,768,3072]{2,0,1:T(1,128)}) %all-reduce.25.cloned.1.call-update) | async-done | bytes 9437200
  1500.1 4.3 dynamic-slice_reduce_fusion
  1508.9 23.3 %bitcast_reduce_fusion = (f32[192,96]{0,1:T(8,128)S(1)}, f32[192,96]{0,1:T(8,128)S(1)}, f32[96,192,128]{2,1,0:T(8,128)S(1)}) fusion(f32[192,96]{0,1:T(8,128)S(1)} %copy-done.43, f32[192,96]{0,1:T(8,128)S(1)} %copy-done.38, bf16[1,192,96,128]{3,2,1,0:T(8,128)(2,1)} %param.32, f32[96,16,192]{2,1,0:T(8,128)S(1)} %reshape.298, bf16[128,16]{0,1:T(8,128)(2,1)S(1)} %copy-done.67), kind=kOutput, calls=%fused_computation.83 | convolution fusion | flops 467103744 | bytes 15634432 | tf_op jit(solution)/shard_map/sjhq,ch->sqjc/dot_general | solution.py:382
  1532.2 11.2 fusion.66
  1543.5 9.2 copy.126
  1556.4 18.9 %all-reduce.17 = (bf16[8,4,96]{2,0,1:T(8,128)(2,1)S(1)}, bf16[8,4,48]{2,0,1:T(8,128)(2,1)S(1)}, bf16[8,4,24]{2,0,1:T(8,128)(2,1)S(1)}) all-reduce(bf16[8,4,96]{2,0,1:T(8,128)(2,1)S(1)} %copy.120, bf16[8,4,48]{2,0,1:T(8,128)(2,1)S(1)} %copy.122, bf16[8,4,24]{2,0,1:T(8,128)(2,1)S(1)} %copy.124), channel_id=8, replica_groups=mesh['samp'=8,'tok'=4] {'tok'}, use_global_device_ids=true, to_apply=%region_36.38.clone | all-reduce | flops 5376 | bytes 21504
  1577.3 22.3 %all-reduce.15 = (f32[8,1,96]{2,1,0:T(1,128)S(1)}, f32[8,1,48]{2,1,0:T(1,128)S(1)}, f32[8,1,24]{2,1,0:T(1,128)S(1)}) all-reduce(f32[8,1,96]{2,1,0:T(1,128)S(1)} %bitcast.318, f32[8,1,48]{2,1,0:T(1,128)S(1)} %bitcast.319, f32[8,1,24]{2,1,0:T(1,128)S(1)} %bitcast.320), channel_id=9, replica_groups=mesh['samp'=8,'tok'=4] {'samp'}, use_global_device_ids=true, to_apply=%region_37.39.clone | all-reduce | flops 1344 | bytes 10752
  1599.6 11.2 fusion.144
  1610.8 38.1 %psum.15 = f32[128,16]{0,1:T(8,128)} all-reduce(f32[128,16]{0,1:T(8,128)S(1)} %fusion.144), channel_id=1, replica_groups=mesh['samp'=8,'tok'=4] {'samp','tok'}, use_global_device_ids=true, to_apply=%region_51.53 | all-reduce | flops 2048 | bytes 16384 | tf_op jit(solution)/shard_map/psum | solution.py:386
  1652.3 17.4 reduce-scatter.22.cloned.1.call-done
  1669.7 38.2 %reduce-scatter.28.cloned.1.call-done = f32[1,1,24,768]{3,2,1,0:T(8,128)} async-done(((f32[8,1,24,768]{3,2,1,0:T(8,128)}), f32[1,1,24,768]{3,2,1,0:T(8,128)}) %reduce-scatter.28.cloned.1.call-update) | async-done | bytes 73744 | tf_op jit(solution)/shard_map/reduce_scatter | solution.py:431
  1707.9 40.8 %reduce-scatter.32.cloned.1.call-done = f32[1,1,48,768]{3,2,1,0:T(8,128)} async-done(((f32[8,1,48,768]{3,2,1,0:T(8,128)}), f32[1,1,48,768]{3,2,1,0:T(8,128)}) %reduce-scatter.32.cloned.1.call-update) | async-done | bytes 147472 | tf_op jit(solution)/shard_map/reduce_scatter | solution.py:433
  1748.7 43.2 %reduce-scatter.24.cloned.1.call-done = f32[384,1,1,144]{0,3,2,1:T(8,128)} async-done(((f32[384,8,1,144]{0,3,2,1:T(8,128)}), f32[384,1,1,144]{0,3,2,1:T(8,128)}) %reduce-scatter.24.cloned.1.call-update) | async-done | bytes 221200 | tf_op jit(solution)/shard_map/reduce_scatter | solution.py:426
  1791.9 46.3 %reduce-scatter.26.cloned.1.call-done = f32[1,1,24,3072]{3,2,1,0:T(8,128)} async-done(((f32[8,1,24,3072]{3,2,1,0:T(8,128)}), f32[1,1,24,3072]{3,2,1,0:T(8,128)}) %reduce-scatter.26.cloned.1.call-update) | async-done | bytes 294928 | tf_op jit(solution)/shard_map/reduce_scatter | solution.py:429
  1838.2 46.8 %reduce-scatter.30.cloned.1.call-done = f32[1,1,24,3072]{3,2,1,0:T(8,128)} async-done(((f32[8,1,24,3072]{3,2,1,0:T(8,128)}), f32[1,1,24,3072]{3,2,1,0:T(8,128)}) %reduce-scatter.30.cloned.1.call-update) | async-done | bytes 294928 | tf_op jit(solution)/shard_map/reduce_scatter | solution.py:432
  (430 shorter events, 203.7 us)
Async XLA Ops:
  7.2 69.8 %copy-start = (f32[256,384]{1,0:T(8,128)S(1)}, f32[256,384]{1,0:T(8,128)}, u32[]{:S(2)}) copy-start(f32[256,384]{1,0:T(8,128)} %param.29) | copy-start | bytes 1179652
  7.2 71.2 %all-gather.9.cloned.1.call-start = ((), (), s32[]{:S(2)}) async-start(), calls=%async_computation.8 | async-start | bytes 3649536 | tf_op jit(solution)/shard_map/all_gather | solution.py:103
  7.9 131.5 %all-gather.11.cloned.1.call-start = ((), (), s32[]{:S(2)}) async-start(), calls=%async_computation.9 | async-start | bytes 4866048 | tf_op jit(solution)/shard_map/all_gather | solution.py:106
  8.7 171.0 %all-gather.17.cloned.1.call-start = ((), (), s32[]{:S(2)}) async-start(), calls=%async_computation.12 | async-start | bytes 5308416 | tf_op jit(solution)/shard_map/all_gather | solution.py:154
  8.7 5.9 copy-start.12
  14.6 8.6 copy-start.37
  14.6 9.2 copy-start.66
  23.9 9.8 copy-start.68
  23.9 10.0 copy-start.69
  23.9 10.3 copy-start.70
  23.9 53.2 %copy-start.60 = (s32[2]{0:T(128)S(1)}, s32[2]{0:T(128)}, u32[]{:S(2)}) copy-start(s32[2]{0:T(128)} %param.30) | copy-start | bytes 28
  31.9 45.4 %copy-start.46 = (bf16[1,192,384]{2,1,0:T(8,128)(2,1)S(1)}, bf16[1,192,384]{2,1,0:T(8,128)(2,1)}, u32[]{:S(2)}) copy-start(bf16[1,192,384]{2,1,0:T(8,128)(2,1)} %param.28) | copy-start | bytes 442372
  31.9 45.9 %copy-start.20 = (bf16[2,192,768]{2,1,0:T(8,128)(2,1)S(1)}, bf16[2,192,768]{2,1,0:T(8,128)(2,1)}, u32[]{:S(2)}) copy-start(bf16[2,192,768]{2,1,0:T(8,128)(2,1)} %param.26) | copy-start | bytes 1769476
  33.5 198.7 %all-gather.15.cloned.1.call-start = ((), (), s32[]{:S(2)}) async-start(), calls=%async_computation.11 | async-start | bytes 2949120 | tf_op jit(solution)/shard_map/all_gather | solution.py:158
  77.3 5.2 copy-start.15
  85.8 60.1 %copy-start.34 = (bf16[2,192,768]{2,1,0:T(8,128)(2,1)}, bf16[2,192,768]{2,1,0:T(8,128)(2,1)S(1)}, u32[]{:S(2)}) copy-start(bf16[2,192,768]{2,1,0:T(8,128)(2,1)S(1)} %fusion.107) | copy-start | bytes 1769476
  147.1 135.9 %all-gather.13.cloned.1.call-start = ((), (), s32[]{:S(2)}) async-start(), calls=%async_computation.10 | async-start | bytes 2949120 | tf_op jit(solution)/shard_map/all_gather | solution.py:159
  147.6 190.9 %all-gather.19.cloned.1.call-start = ((), (), s32[]{:S(2)}) async-start(), calls=%async_computation.13 | async-start | bytes 1216512 | tf_op jit(solution)/shard_map/all_gather | solution.py:108
  148.2 255.7 %all-gather.21.cloned.1.call-start = ((), (), s32[]{:S(2)}) async-start(), calls=%async_computation.14 | async-start | bytes 4866048 | tf_op jit(solution)/shard_map/all_gather | solution.py:109
  149.0 313.9 %all-gather.23.cloned.1.call-start = ((), (), s32[]{:S(2)}) async-start(), calls=%async_computation.15 | async-start | bytes 2433024 | tf_op jit(solution)/shard_map/all_gather | solution.py:110
  149.7 572.2 %reduce-scatter.20.cloned.1.call-start = ((), (), s32[]{:S(2)}) async-start(), calls=%async_computation.17 | async-start | bytes 2949120 | tf_op jit(solution)/shard_map/reduce_scatter | solution.py:324
  275.6 10.2 copy-start.6
  320.0 6.7 copy-start.19
  342.4 132.1 %copy-start.17 = (f32[2,192,768]{2,1,0:T(8,128)}, f32[2,192,768]{2,1,0:T(8,128)S(1)}, u32[]{:S(2)}) copy-start(f32[2,192,768]{2,1,0:T(8,128)S(1)} %get-tuple-element.831) | copy-start | bytes 3538948
  342.4 132.1 %copy-start.51 = (f32[2,192]{1,0:T(2,128)}, f32[2,192]{1,0:T(2,128)S(1)}, u32[]{:S(2)}) copy-start(f32[2,192]{1,0:T(2,128)S(1)} %broadcast_multiply_fusion.7) | copy-start | bytes 4612
  342.7 131.8 %copy-start.53 = (f32[2,192]{1,0:T(2,128)}, f32[2,192]{1,0:T(2,128)S(1)}, u32[]{:S(2)}) copy-start(f32[2,192]{1,0:T(2,128)S(1)} %add_rsqrt_fusion.1) | copy-start | bytes 4612
  462.9 6.2 copy-start.27
  469.1 5.4 copy-start.75
  469.1 5.4 copy-start.77
  528.8 5.5 copy-start.2
  528.8 6.0 copy-start.22
  536.9 5.5 copy-start.23
  542.4 23.2 %copy-start.26 = (bf16[2,768,16,48]{1,3,2,0:T(8,128)(2,1)}, bf16[2,768,16,48]{1,3,2,0:T(8,128)(2,1)S(1)}, u32[]{:S(2)}) copy-start(bf16[2,768,16,48]{1,3,2,0:T(8,128)(2,1)S(1)} %bitcast_dynamic-update-slice_fusion.5) | copy-start | bytes 7077892 | tf_op jit(solution)/shard_map/while
  579.7 5.9 copy-start.2
  579.7 6.5 copy-start.22
  588.2 5.5 copy-start.23
  593.7 23.2 %copy-start.26 = (bf16[2,768,16,48]{1,3,2,0:T(8,128)(2,1)}, bf16[2,768,16,48]{1,3,2,0:T(8,128)(2,1)S(1)}, u32[]{:S(2)}) copy-start(bf16[2,768,16,48]{1,3,2,0:T(8,128)(2,1)S(1)} %bitcast_dynamic-update-slice_fusion.5) | copy-start | bytes 7077892 | tf_op jit(solution)/shard_map/while
  631.0 5.9 copy-start.2
  631.0 6.5 copy-start.22
  639.6 5.5 copy-start.23
  645.1 23.2 %copy-start.26 = (bf16[2,768,16,48]{1,3,2,0:T(8,128)(2,1)}, bf16[2,768,16,48]{1,3,2,0:T(8,128)(2,1)S(1)}, u32[]{:S(2)}) copy-start(bf16[2,768,16,48]{1,3,2,0:T(8,128)(2,1)S(1)} %bitcast_dynamic-update-slice_fusion.5) | copy-start | bytes 7077892 | tf_op jit(solution)/shard_map/while
  674.8 96.8 %reduce-scatter.18.cloned.1.call-start = ((), (), s32[]{:S(2)}) async-start(), calls=%async_computation.16 | async-start | bytes 2949120 | tf_op jit(solution)/shard_map/reduce_scatter | solution.py:318
  678.9 680.7 %all-reduce.27.cloned.1.call-start = ((), (), s32[]{:S(2)}) async-start(), calls=%async_computation.26 | async-start | bytes 33030144
  686.9 84.7 %copy-start.21 = (bf16[2,192,768]{2,1,0:T(8,128)(2,1)S(1)}, bf16[2,192,768]{2,1,0:T(8,128)(2,1)}, u32[]{:S(2)}) copy-start(bf16[2,192,768]{2,1,0:T(8,128)(2,1)} %param.26) | copy-start | bytes 1769476
  687.0 84.7 %copy-start.56 = (f32[2,192]{1,0:T(2,128)S(1)}, f32[2,192]{1,0:T(2,128)}, u32[]{:S(2)}) copy-start(f32[2,192]{1,0:T(2,128)} %copy-done.55) | copy-start | bytes 4612
  687.0 84.7 %copy-start.58 = (f32[2,192]{1,0:T(2,128)S(1)}, f32[2,192]{1,0:T(2,128)}, u32[]{:S(2)}) copy-start(f32[2,192]{1,0:T(2,128)} %copy-done.57) | copy-start | bytes 4612
  687.0 84.7 %copy-start.74 = (bf16[2,192,768]{2,1,0:T(8,128)(2,1)S(1)}, bf16[2,192,768]{2,1,0:T(8,128)(2,1)}, u32[]{:S(2)}) copy-start(bf16[2,192,768]{2,1,0:T(8,128)(2,1)} %get-tuple-element.842) | copy-start | bytes 1769476
  771.6 5.9 slice-start.2
  771.7 5.9 slice-start.3
  791.8 5.9 copy-start.35
  791.8 5.9 copy-start.64
  791.8 5.9 copy-start.65
  802.5 697.7 %all-reduce.25.cloned.1.call-start = ((), (), s32[]{:S(2)}) async-start(), calls=%async_computation.25 | async-start | bytes 18874368
  823.4 7.0 copy-start.61
  823.4 828.9 %all-reduce.23.cloned.1.call-start = ((), (), s32[]{:S(2)}) async-start(), calls=%async_computation.19 | async-start | bytes 786432 | tf_op jit(solution)/shard_map/psum | solution.py:386
  831.7 838.0 %reduce-scatter.22.cloned.1.call-start = ((), (), s32[]{:S(2)}) async-start(), calls=%async_computation.18 | async-start | bytes 442368 | tf_op jit(solution)/shard_map/reduce_scatter | solution.py:376
  834.2 873.8 %reduce-scatter.28.cloned.1.call-start = ((), (), s32[]{:S(2)}) async-start(), calls=%async_computation.22 | async-start | bytes 663552 | tf_op jit(solution)/shard_map/reduce_scatter | solution.py:431
  1362.1 386.6 %reduce-scatter.32.cloned.1.call-start = ((), (), s32[]{:S(2)}) async-start(), calls=%async_computation.24 | async-start | bytes 1327104 | tf_op jit(solution)/shard_map/reduce_scatter | solution.py:433
  1365.0 426.9 %reduce-scatter.24.cloned.1.call-start = ((), (), s32[]{:S(2)}) async-start(), calls=%async_computation.20 | async-start | bytes 1990656 | tf_op jit(solution)/shard_map/reduce_scatter | solution.py:426
  1368.3 469.9 %reduce-scatter.26.cloned.1.call-start = ((), (), s32[]{:S(2)}) async-start(), calls=%async_computation.21 | async-start | bytes 2654208 | tf_op jit(solution)/shard_map/reduce_scatter | solution.py:429
  1372.0 513.0 %reduce-scatter.30.cloned.1.call-start = ((), (), s32[]{:S(2)}) async-start(), calls=%async_computation.23 | async-start | bytes 2654208 | tf_op jit(solution)/shard_map/reduce_scatter | solution.py:432
  1508.8 23.4 %slice-start = ((s8[4718592]{0:T(1024)(128)(4,1)}), s8[524288]{0:T(1024)(128)(4,1)S(1)}, s32[]{:S(2)}) async-start(s8[4718592]{0:T(1024)(128)(4,1)} %bitcast.303), calls=%async_computation.27 | async-start | bytes 1048576
  1508.9 23.3 %slice-start.1 = ((s8[4718592]{0:T(1024)(128)(4,1)}), s8[4194304]{0:T(1024)(128)(4,1)S(1)}, s32[]{:S(2)}) async-start(s8[4718592]{0:T(1024)(128)(4,1)} %bitcast.303), calls=%async_computation.28 | async-start | bytes 8388608
  1599.6 287.1 %copy-start.1 = (f32[256,384]{1,0:T(8,128)S(1)}, f32[256,384]{1,0:T(8,128)}, u32[]{:S(2)}) copy-start(f32[256,384]{1,0:T(8,128)} %param.29) | copy-start | bytes 1179652
  (62 other events, 186.4 us)
Sparse Core Ops, SparseCore 0:
  10.8 63.3 all-gather.8
  77.1 62.3 all-gather.10
  141.9 37.7 all-gather.16
  181.7 50.4 all-gather.14
  233.6 49.2 all-gather.12
  285.6 52.8 all-gather.18
  341.4 62.4 all-gather.20
  406.7 56.1 all-gather.22
  674.9 46.9 reduce-scatter.19
  724.1 47.5 reduce-scatter.17
  802.6 556.9 all-reduce.26
  1363.3 136.7 all-reduce.24
  1505.4 127.4 all-reduce.22
  1636.7 32.8 reduce-scatter.21
  1673.5 34.3 reduce-scatter.27
  1711.9 36.7 reduce-scatter.31
  1752.5 39.3 reduce-scatter.23
  1795.7 42.4 reduce-scatter.25
  1842.5 42.4 reduce-scatter.29
where the time goes:
time: 1900 us; the launch traced here: 1890 us
  waiting for transfers between devices  1220 us (64%)
  matrix products  293 us (15%)
  local copies, waits for them, and re-layouts  122 us (6%)
  blocking collectives  122 us (6%)
  other arithmetic  105 us (6%)
    unnamed x21, waiting for transfers between devices  656 us
    unnamed x3, blocking collectives  83.9 us
    dot_general x3, matrix products, grad_pass(): jnp.einsum('as,akhq->skhq', chooser, logits_back, precision=highest)  69.5 us
    all_gather x1, waiting for transfers between devices, per_device(): lax.all_gather(expander, ('samp', 'tok'), axis=0, tiled=True)  57.6 us
    all_gather x1, waiting for transfers between devices, per_device(): lax.all_gather(projector, ('samp', 'tok'), axis=0, tiled=True)  53.7 us
    all_gather x1, waiting for transfers between devices, per_device(): lax.all_gather(reducer, ('samp', 'tok'), axis=0, tiled=True)  52.3 us
    reduce_scatter x1, waiting for transfers between devices, per_device(): lax.psum_scatter(keys_back.reshape(S_DEV, N, D).astype(jnp.bfloat16), 'to...  49.7 us
    reduce_scatter x1, waiting for transfers between devices, per_device(): lax.psum_scatter(sectioned[6], 'samp', scatter_dimension=0, tiled=True)  46.8 us
  transfers between devices with their start and end apart: 19, of which 17 were waited for; matrix products, arithmetic and copies ran while one was open for 14% of the time, Pallas kernels for 0%

commit v1 on v0

v1 whole, which is shorter than its diff:
```python
import jax
import jax.numpy as jnp
from jax import lax
from jax.experimental import pallas as pl
from jax.experimental.pallas import tpu as pltpu
from jax.sharding import PartitionSpec as P
DH=48; EPS=1e-5; WIN=256
f32=jnp.float32; bf16=jnp.bfloat16
NT=(((1,),(1,)),((),()))
TN=(((0,),(0,)),((),()))
VL=56*1024*1024

def _window(h, width):
    w = jnp.minimum((h * DH) // 128 * 128, width - WIN)
    w = pl.multiple_of(w, 128)
    lane = lax.broadcasted_iota(jnp.int32, (1, WIN), 1) + w
    return w, (lane >= h * DH) & (lane < h * DH + DH)

def _attn_fwd(q_ref, k_ref, v_ref, bias_ref, mask_ref, p_ref, att_ref):
    h = pl.program_id(0)
    samples, _, width = q_ref.shape
    w, inside = _window(h, width)
    bias = bias_ref[0].astype(f32) + mask_ref[...]
    for b in range(samples):
        q = jnp.where(inside, q_ref[b, :, pl.ds(w, WIN)], 0)
        s = lax.dot_general(q, k_ref[b, :, pl.ds(w, WIN)], NT, preferred_element_type=f32)
        s = s * (DH ** -0.5) + bias
        e = jnp.exp(s - jnp.max(s, axis=1, keepdims=True))
        p = (e * (1.0 / jnp.sum(e, axis=1, keepdims=True))).astype(bf16)
        p_ref[0, b] = p
        o = jnp.dot(p, v_ref[b, :, pl.ds(w, WIN)], preferred_element_type=f32)
        att_ref[b, :, pl.ds(w, WIN)] = jnp.where(inside, o, att_ref[b, :, pl.ds(w, WIN)])

def attn_fwd(q, k, v, bias, mask):
    S, R, D = q.shape; N = k.shape[1]; H = bias.shape[0]
    whole = lambda shape: pl.BlockSpec(shape, lambda h: (0,) * len(shape))
    return pl.pallas_call(
        _attn_fwd, grid=(H,),
        in_specs=[whole((S, R, D)), whole((S, N, D)), whole((S, N, D)),
                  pl.BlockSpec((1, R, N), lambda h: (h, 0, 0)), whole((1, N))],
        out_specs=[pl.BlockSpec((1, S, R, N), lambda h: (h, 0, 0, 0)), whole((S, R, D))],
        out_shape=[jax.ShapeDtypeStruct((H, S, R, N), bf16), jax.ShapeDtypeStruct((S, R, D), f32)],
        compiler_params=pltpu.CompilerParams(vmem_limit_bytes=VL),
        cost_estimate=pl.CostEstimate(flops=4*S*H*R*N*WIN, bytes_accessed=20_000_000, transcendentals=S*H*R*N),
        name="attention",
    )(q, k, v, bias, mask)

def _attn_bwd(p_ref, do_ref, k_ref, v_ref, qt_ref, dot_ref, dq_ref, dkt_ref, dvt_ref, bb_ref):
    h = pl.program_id(0)
    samples, _, width = do_ref.shape
    w, inside = _window(h, width)
    acc = None
    for b in range(samples):
        do = jnp.where(inside, do_ref[b, :, pl.ds(w, WIN)], 0)
        dp = lax.dot_general(do, v_ref[b, :, pl.ds(w, WIN)], NT, preferred_element_type=f32)
        pl_ = p_ref[0, b]
        p = pl_.astype(f32)
        ds = p * (dp - jnp.sum(p * dp, axis=1, keepdims=True))
        acc = ds if acc is None else acc + ds
        dsl = ds.astype(bf16)
        dq = jnp.dot(dsl, k_ref[b, :, pl.ds(w, WIN)], preferred_element_type=f32) * (DH ** -0.5)
        dq_ref[b, :, pl.ds(w, WIN)] = jnp.where(inside, dq, dq_ref[b, :, pl.ds(w, WIN)])
        dkt_ref[b] = (jnp.dot(qt_ref[b], dsl, preferred_element_type=f32) * (DH ** -0.5)).astype(bf16)
        dvt_ref[b] = jnp.dot(dot_ref[b], pl_, preferred_element_type=f32).astype(bf16)
    bb_ref[0] = acc.astype(bb_ref.dtype)

def attn_bwd(p, do, k, v, qt, dot_):
    H, S, R, N = p.shape; D = do.shape[2]
    whole = lambda shape: pl.BlockSpec(shape, lambda h: (0,) * len(shape))
    return pl.pallas_call(
        _attn_bwd, grid=(H,),
        in_specs=[pl.BlockSpec((1, S, R, N), lambda h: (h, 0, 0, 0)), whole((S, R, D)), whole((S, N, D)), whole((S, N, D)),
                  pl.BlockSpec((S, DH, R), lambda h: (0, h, 0)), pl.BlockSpec((S, DH, R), lambda h: (0, h, 0))],
        out_specs=[whole((S, R, D)), pl.BlockSpec((S, DH, N), lambda h: (0, h, 0)), pl.BlockSpec((S, DH, N), lambda h: (0, h, 0)),
                   pl.BlockSpec((1, R, N), lambda h: (h, 0, 0))],
        out_shape=[jax.ShapeDtypeStruct((S, R, D), f32), jax.ShapeDtypeStruct((S, D, N), bf16), jax.ShapeDtypeStruct((S, D, N), bf16),
                   jax.ShapeDtypeStruct((H, R, N), bf16)],
        compiler_params=pltpu.CompilerParams(vmem_limit_bytes=VL),
        cost_estimate=pl.CostEstimate(flops=8*S*H*R*N*WIN, bytes_accessed=30_000_000, transcendentals=0),
        name="attention_back",
    )(p, do, k, v, qt, dot_)

def _normal(x):
    c = x - jnp.mean(x, axis=-1, keepdims=True)
    r = lax.rsqrt(jnp.mean(c * c, axis=-1, keepdims=True) + EPS)
    return c * r, r

def _pair_fwd(x_ref, ph_ref, out_ref, buf):
    n = x_ref.shape[0]
    ph = ph_ref[...]
    for i in range(n):
        nrm, _ = _normal(x_ref[i].astype(f32))
        buf[:, i, :] = lax.dot_general(ph, nrm.astype(bf16), NT, preferred_element_type=f32)
    out_ref[...] = buf[...].astype(bf16)

def pair_fwd(x, pht, blk=16):
    R, C, E = x.shape; H = pht.shape[0]
    return pl.pallas_call(
        _pair_fwd, grid=(R // blk,),
        in_specs=[pl.BlockSpec((blk, C, E), lambda i: (i, 0, 0)), pl.BlockSpec((H, E), lambda i: (0, 0))],
        out_specs=pl.BlockSpec((H, blk, C), lambda i: (0, i, 0)),
        out_shape=jax.ShapeDtypeStruct((H, R, C), bf16),
        scratch_shapes=[pltpu.VMEM((H, blk, C), f32)],
        compiler_params=pltpu.CompilerParams(vmem_limit_bytes=VL),
        cost_estimate=pl.CostEstimate(flops=2*R*C*E*H, bytes_accessed=2*R*C*E, transcendentals=R*C),
        name="pair_bias",
    )(x, pht)

def _split(x):
    hi = x.astype(bf16)
    return jnp.concatenate([hi, (x - hi.astype(f32)).astype(bf16)], axis=0)

def _pair_bwd(x_ref, bb_ref, ph_ref, out_ref, dph_ref):
    n = x_ref.shape[0]
    H = ph_ref.shape[0]
    ph2 = jnp.concatenate([ph_ref[...], ph_ref[...]], axis=0)
    acc = jnp.zeros((2 * H, ph_ref.shape[1]), f32)
    for i in range(n):
        nrm, r = _normal(x_ref[i].astype(f32))
        b2 = _split(bb_ref[i])
        g = lax.dot_general(b2, ph2, TN, preferred_element_type=f32)
        m1 = jnp.mean(g, axis=-1, keepdims=True)
        m2 = jnp.mean(g * nrm, axis=-1, keepdims=True)
        out_ref[i] = r * (g - m1 - nrm * m2)
        acc += jnp.dot(b2, nrm.astype(bf16), preferred_element_type=f32)
    part = acc[:H] + acc[H:]
    @pl.when(pl.program_id(0) == 0)
    def _(): dph_ref[...] = part
    @pl.when(pl.program_id(0) != 0)
    def _(): dph_ref[...] += part

def pair_bwd(x, bb, pht, blk=16):
    R, C, E = x.shape; H = pht.shape[0]
    return pl.pallas_call(
        _pair_bwd, grid=(R // blk,),
        in_specs=[pl.BlockSpec((blk, C, E), lambda i: (i, 0, 0)), pl.BlockSpec((blk, H, C), lambda i: (i, 0, 0)), pl.BlockSpec((H, E), lambda i: (0, 0))],
        out_specs=[pl.BlockSpec((blk, C, E), lambda i: (i, 0, 0)), pl.BlockSpec((H, E), lambda i: (0, 0))],
        out_shape=[jax.ShapeDtypeStruct((R, C, E), f32), jax.ShapeDtypeStruct((H, E), f32)],
        compiler_params=pltpu.CompilerParams(vmem_limit_bytes=VL),
        cost_estimate=pl.CostEstimate(flops=8*R*C*E*H, bytes_accessed=6*R*C*E, transcendentals=R*C),
        name="pair_back",
    )(x, bb, pht)

def normal_rows(x):
    c = x - jnp.mean(x, axis=-1, keepdims=True)
    r = lax.rsqrt(jnp.mean(c * c, axis=-1, keepdims=True) + EPS)
    return c * r, r


def norm_back(n, r, g):
    return r * (g - jnp.mean(g, axis=-1, keepdims=True) - n * jnp.mean(g * n, axis=-1, keepdims=True))


def slope(s):
    return s * (1.0 - s)


def mm(a, b, ca, cb, out=f32):
    return lax.dot_general(a, b, ((ca, cb), ((), ())), preferred_element_type=f32).astype(out)


def hop(x, axis, k):
    n = lax.axis_size(axis)
    return lax.ppermute(x, axis, [(i, i ^ k) for i in range(n)])


def at(x, i):
    return lax.dynamic_index_in_dim(x, i, 0, keepdims=False)


def gather_tok(x):
    n = lax.axis_size("tok")
    if n & (n - 1):
        return lax.all_gather(x, "tok", axis=0)
    t = lax.axis_index("tok")
    out = jnp.zeros((n,) + x.shape, x.dtype)
    out = lax.dynamic_update_slice_in_dim(out, x[None], t, 0)
    for k in range(1, n):
        out = lax.dynamic_update_slice_in_dim(out, hop(x, "tok", k)[None], t ^ k, 0)
    return out


def sum_tok(x):
    n = lax.axis_size("tok")
    if n & (n - 1):
        return lax.psum_scatter(x.astype(bf16), "tok", scatter_dimension=0, tiled=False).astype(f32)
    t = lax.axis_index("tok")
    total = at(x, t).astype(f32)
    for k in range(1, n):
        total = total + hop(at(x, t ^ k).astype(bf16), "tok", k).astype(f32)
    return total


def sum_samp(parts):
    n = lax.axis_size("samp")
    if n != 8:
        whole = jnp.concatenate([p.astype(bf16) for p in parts], axis=-2)
        return lax.psum_scatter(whole, "samp", scatter_dimension=0, tiled=False).astype(f32)
    s = lax.axis_index("samp")
    j, c = s // 2, s % 2

    def half(which):
        picked = [
            lax.dynamic_index_in_dim(p.reshape((n // 2, 2) + p.shape[1:]), which, 1, keepdims=False)
            for p in parts
        ]
        return jnp.concatenate(picked, axis=-2) if len(picked) > 1 else picked[0]

    both = half(c).astype(f32) + hop(half(1 - c).astype(bf16), "samp", 1).astype(f32)
    both = both.astype(bf16)
    total = at(both, j).astype(f32)
    for k in range(1, n // 2):
        total = total + hop(at(both, j ^ k), "samp", 2 * k).astype(f32)
    return total


def per_device(
    tokens_in, cotangent, singles, noise_table, noise_level, pad_mask, pairwise, conditioner,
    offsets, shifts, projector, querybias, combiner, expander, reducer, pairhead,
):
    S, R, D = tokens_in.shape
    C = pairwise.shape[2]
    N = pad_mask.shape[1]
    H = pairhead.shape[1]
    CS = conditioner.shape[0]
    T = lax.axis_size("tok")
    G = lax.axis_size("samp")
    t = lax.axis_index("tok")
    scale_dot = DH ** -0.5

    def blocks(w):
        return [w[:, i * D : (i + 1) * D] for i in range(w.shape[1] // D)]

    cc = conditioner.shape[1]
    cond_t = conditioner.T
    pr = projector.shape[0]
    rr = reducer.shape[0]
    vec = jnp.concatenate([offsets, shifts, querybias])
    vec_row = jnp.zeros((8, D), bf16).at[0, : vec.shape[0]].set(vec)
    cond_rows = jnp.concatenate([cond_t[: cc // 2], cond_t[cc // 2 :]], axis=1)
    first = jnp.concatenate(blocks(projector) + [cond_rows, vec_row], axis=0)
    second = jnp.concatenate(blocks(expander) + [combiner, reducer], axis=0)
    first_all = lax.all_gather(first, ("samp", "tok"), axis=0)
    second_all = lax.all_gather(second, ("samp", "tok"), axis=0)
    W = G * T

    def rows_of(buf, start, count):
        return buf[:, start : start + count].reshape(W * count, D)

    proj_full = jnp.concatenate([rows_of(first_all, i * pr, pr) for i in range(4)], axis=1)
    cond_full = first_all[:, 4 * pr : 4 * pr + cc // 2]
    cond_full = jnp.concatenate([cond_full[:, :, :CS], cond_full[:, :, CS:]], axis=1).reshape(W * cc, CS)
    vecs = first_all[:, 4 * pr + cc // 2].astype(f32)
    no, ns = offsets.shape[0], shifts.shape[0]
    o = jnp.split(vecs[:, :no].reshape(W * no), 4)
    sh = jnp.split(vecs[:, no : no + ns].reshape(W * ns), 2)
    querybias_full = vecs[:, no + ns : no + ns + pr].reshape(W * pr)
    expand_full = jnp.concatenate([rows_of(second_all, i * pr, pr) for i in range(4)], axis=1)
    comb_full = rows_of(second_all, 4 * pr, pr)
    reduce_full = rows_of(second_all, 5 * pr, rr)

    pht = pairhead.T
    piece = pair_fwd(pairwise[0], pht)
    bias_all = jnp.transpose(lax.all_gather(piece, "samp", axis=0), (1, 2, 0, 3)).reshape(H, R, N)
    mask_add = (pad_mask.astype(f32) - 1.0) * 1e9

    singles_rows = jnp.concatenate([singles[0, : R // 2], singles[0, R // 2 :]], axis=1)
    mine = jnp.concatenate([tokens_in.reshape(S * R, D), singles_rows], axis=0)
    every = gather_tok(mine)
    tokens_all = every[:, : S * R].reshape(T, S, R, D).transpose(1, 0, 2, 3).reshape(S, N, D)
    halves = every[:, S * R :]
    singles_all = jnp.concatenate([halves[:, :, :CS], halves[:, :, CS:]], axis=1).reshape(N, CS)

    noise_rows = jnp.stack([at(noise_table, noise_level[b]) for b in range(S)])
    cond_norm_all, cond_inv_all = normal_rows(singles_all.astype(f32)[None] + noise_rows[:, None])
    cond_low_all = cond_norm_all.astype(bf16)

    def own(x):
        return lax.dynamic_slice_in_dim(x, t * R, R, 1)

    adapt_pre = mm(cond_low_all, cond_full[: 2 * D], (2,), (1,)) + jnp.concatenate([o[0], sh[0]])
    cond_norm, cond_inv = normal_rows(singles.astype(f32) + noise_rows[:, None])
    cond_low = cond_norm.astype(bf16)
    adapt_own = mm(cond_low, cond_full[2 * D :], (2,), (1,)) + jnp.concatenate([o[1], o[2], sh[1], o[3]])
    pregate, postscale, postshift, postgate = jnp.split(adapt_own, 4, axis=-1)

    token_norm_all, token_inv_all = normal_rows(tokens_all.astype(f32))
    gain_all = jax.nn.sigmoid(adapt_pre[..., :D])
    pre_all = (gain_all * token_norm_all + adapt_pre[..., D:]).astype(bf16)
    pre = own(pre_all)
    keys = mm(pre_all, proj_full[:, D : 2 * D], (2,), (0,), bf16)
    values = mm(pre_all, proj_full[:, 2 * D : 3 * D], (2,), (0,), bf16)
    query = (mm(pre, proj_full[:, :D], (2,), (0,)) + querybias_full).astype(bf16)
    gating = jax.nn.sigmoid(mm(pre, proj_full[:, 3 * D :], (2,), (0,)))

    probs, attended = attn_fwd(query, keys, values, bias_all, mask_add)

    tokens = tokens_in.astype(f32)
    gated = (gating * attended).astype(bf16)
    branch = mm(gated, comb_full, (2,), (0,))
    pregate_sig = jax.nn.sigmoid(pregate)
    residual = tokens + pregate_sig * branch
    post_norm, post_inv = normal_rows(residual)
    post_gain = jax.nn.sigmoid(postscale)
    posthidden = (post_gain * post_norm + postshift).astype(bf16)
    upgate = mm(posthidden, expand_full, (2,), (0,))
    FF = upgate.shape[-1] // 2
    preact, upper = upgate[..., :FF], upgate[..., FF:]
    preact_sig = jax.nn.sigmoid(preact)
    swished = preact * preact_sig
    activated = (swished * upper).astype(bf16)
    trans = mm(activated, reduce_full, (2,), (0,))
    postgate_sig = jax.nn.sigmoid(postgate)
    mixed = (residual + postgate_sig * trans).astype(bf16)

    def owned(grad):
        return [
            g.reshape(G, T, g.shape[0] // W, D)
            for g in (grad[:, i * D : (i + 1) * D] for i in range(grad.shape[1] // D))
        ]

    trans_back = (postgate_sig * cotangent).astype(bf16)
    postgate_back = cotangent * trans * slope(postgate_sig)
    reducer_part = mm(activated, trans_back, (0, 1), (0, 1), bf16)
    act_back = mm(trans_back, reduce_full, (2,), (1,))
    up_back = jnp.concatenate(
        [act_back * upper * preact_sig * (1.0 + preact * (1.0 - preact_sig)), act_back * swished], axis=-1
    ).astype(bf16)
    expander_part = mm(posthidden, up_back, (0, 1), (0, 1), bf16)
    posthidden_back = mm(up_back, expand_full, (2,), (1,))
    postscale_back = posthidden_back * post_norm * slope(post_gain)
    residual_back = cotangent + norm_back(post_norm, post_inv, posthidden_back * post_gain)
    branch_back = (pregate_sig * residual_back).astype(bf16)
    pregate_back = residual_back * branch * slope(pregate_sig)
    combiner_part = mm(gated, branch_back, (0, 1), (0, 1), bf16)
    second_sum = sum_tok(
        sum_samp(
            [
                p.reshape(G, -1, D)
                for p in [jnp.concatenate(owned(expander_part) + owned(combiner_part) + owned(reducer_part), axis=2)]
            ]
        ).reshape(T, -1, D)
    )

    gated_back = mm(branch_back, comb_full, (2,), (1,))
    attended_back = (gating * gated_back).astype(bf16)
    gating_back = attended * gated_back * slope(gating)
    query_back, keys_back_t, values_back_t, bias_back = attn_bwd(
        probs, attended_back, keys, values, query.transpose(0, 2, 1), attended_back.transpose(0, 2, 1)
    )
    bias_sum = sum_samp([bias_back.reshape(H * R, G, C).transpose(1, 0, 2)]).reshape(H, R, C)
    pair_grad, pairhead_part = pair_bwd(pairwise[0], bias_sum.transpose(1, 0, 2), pht)

    query_low = query_back.astype(bf16)
    gating_low = gating_back.astype(bf16)
    pre_back_all = mm(keys_back_t, proj_full[:, D : 2 * D], (1,), (1,)) + mm(
        values_back_t, proj_full[:, 2 * D : 3 * D], (1,), (1,)
    )
    pre_back = sum_tok(pre_back_all.astype(bf16).reshape(S, T, R, D).transpose(1, 0, 2, 3))
    pre_back = pre_back + mm(query_low, proj_full[:, :D], (2,), (1,)) + mm(gating_low, proj_full[:, 3 * D :], (2,), (1,))
    projector_parts = [
        mm(pre, query_low, (0, 1), (0, 1), bf16),
        mm(pre_all, keys_back_t, (0, 1), (0, 2), bf16),
        mm(pre_all, values_back_t, (0, 1), (0, 2), bf16),
        mm(pre, gating_low, (0, 1), (0, 1), bf16),
    ]
    token_norm, token_inv = normal_rows(tokens)
    gain = jax.nn.sigmoid(own(adapt_pre[..., :D]))
    prescale_back = pre_back * token_norm * slope(gain)
    tokens_grad = residual_back + norm_back(token_norm, token_inv, pre_back * gain)
    adapt_back = jnp.concatenate(
        [prescale_back, pre_back, pregate_back, postscale_back, posthidden_back, postgate_back], axis=-1
    )
    sums = jnp.split(jnp.sum(adapt_back, axis=(0, 1)), 6)
    offsets_part = jnp.concatenate([sums[0], sums[2], sums[3], sums[5]])
    shifts_part = jnp.concatenate([sums[1], sums[4]])
    querybias_part = jnp.sum(query_back, axis=(0, 1))
    adapt_low = adapt_back.astype(bf16)
    cond_part = mm(adapt_low, cond_low, (0, 1), (0, 1), bf16).reshape(G, T, cc, CS)
    cond_part = jnp.concatenate([cond_part[:, :, : cc // 2], cond_part[:, :, cc // 2 :]], axis=-1)
    vec_part = jnp.concatenate(
        [offsets_part.reshape(G, T, no), shifts_part.reshape(G, T, ns), querybias_part.reshape(G, T, pr)], axis=-1
    )
    vec_part = jnp.zeros((G, T, 8, D), bf16).at[:, :, 0, : vec.shape[0]].set(vec_part.astype(bf16))
    first_part = jnp.concatenate([x for p in projector_parts for x in owned(p)] + [cond_part, vec_part], axis=2)
    first_sum = sum_tok(sum_samp([first_part.reshape(G, -1, D)]).reshape(T, -1, D))

    cond_grad = norm_back(cond_norm, cond_inv, mm(adapt_low, cond_full, (2,), (0,)))
    cs = CS // G
    singles_grad = sum_samp([jnp.sum(cond_grad, axis=0).reshape(R, G, cs).transpose(1, 2, 0)]).T[None]
    levels = jnp.arange(noise_table.shape[0], dtype=jnp.int32)
    level_hot = (noise_level[:, None] == levels[None, :]).astype(f32)
    noise_part = jnp.dot(level_hot.T, jnp.sum(cond_grad, axis=1), precision=lax.Precision.HIGHEST)
    noise_grad, pairhead_grad = lax.psum((noise_part, pairhead_part), ("samp", "tok"))

    def unblocks(x):
        return jnp.concatenate([x[i * pr : (i + 1) * pr] for i in range(4)], axis=1)

    projector_grad = unblocks(first_sum)
    cond_out = first_sum[4 * pr : 4 * pr + cc // 2]
    conditioner_grad = jnp.concatenate([cond_out[:, :CS], cond_out[:, CS:]], axis=0).T
    vec_out = first_sum[4 * pr + cc // 2]
    expander_grad = unblocks(second_sum)
    combiner_grad = second_sum[4 * pr : 5 * pr]
    reducer_grad = second_sum[5 * pr :]
    return (
        mixed,
        tokens_grad,
        singles_grad,
        pair_grad[None],
        noise_grad,
        conditioner_grad,
        vec_out[:no],
        vec_out[no : no + ns],
        projector_grad,
        vec_out[no + ns : no + ns + pr],
        combiner_grad,
        expander_grad,
        reducer_grad,
        pairhead_grad.T,
    )


def solution(mesh):
    shard = ("samp", "tok")
    in_specs = (
        P("samp", "tok", None), P("samp", "tok", None), P(None, "tok", None), P(), P("samp"), P(),
        P(None, "tok", "samp", None), P(None, shard), P(shard), P(shard), P(shard, None), P(shard),
        P(shard, None), P(shard, None), P(shard, None), P(),
    )
    out_specs = (
        P("samp", "tok", None), P("samp", "tok", None), P(None, "tok", "samp"), P(None, "tok", "samp", None), P(),
        P(None, shard), P(shard), P(shard), P(shard, None), P(shard), P(shard, None), P(shard, None),
        P(shard, None), P(),
    )
    return jax.shard_map(per_device, mesh=mesh, in_specs=in_specs, out_specs=out_specs, check_vma=False)
```

time: 1900 us -> 744 us (0.39)
  waiting for transfers between devices: 1220 us -> 215 us
  matrix products: 293 us -> 87.1 us
  Pallas kernels: 0 us -> 96.2 us
  blocking collectives: 122 us -> 40.2 us
  local copies, waits for them, and re-layouts: 122 us -> 189 us
  other arithmetic: 105 us -> 57.1 us
  starting transfers between devices: 1.42 us -> 31.7 us
    unnamed x21 -> x4, waiting for transfers between devices: 656 us -> 0.07 us
    reduce_scatter x8 -> x0, waiting for transfers between devices: 313 us -> none  [the longest x1 49.7 us: per_device(): lax.psum_scatter(keys_back.reshape(S_DEV, N, D).astype(jnp.bfloat16), 'to...]
    dot_general x51 -> x26, matrix products: 293 us -> 87.1 us  [the longest x25 85.9 us: mm(): lax.dot_general(a, b, ((ca, cb), ((), ())), preferred_element_type=f32)]
    all_gather x8 -> x3, waiting for transfers between devices: 256 us -> 106 us  [the longest x1 71.9 us: per_device(): first_all = lax.all_gather(first, ('samp', 'tok'), axis=0)]
    ppermute x0 -> x28, waiting for transfers between devices: none -> 109 us  [hop(): return lax.ppermute(x, axis, [(i, i ^ k) for i in range(n)])]
    pallas_call x0 -> x4, Pallas kernels: none -> 96.2 us  [the longest x1 35.7 us: pair_bwd(): pl.pallas_call(_pair_bwd, grid=(R // blk,), in_specs=[pl.BlockSpec((blk,...]
    unnamed x3 -> x0, blocking collectives: 83.9 us -> none
    convert_element_type x28 -> x10, other arithmetic: 59 us -> 16.2 us  [the longest x4 11.5 us: sum_samp(): both = both.astype(bf16)]
  transfers between devices with their start and end apart: 19 -> 32, of which waited for: 17 -> 12; matrix products, arithmetic and copies ran while one was open for 14% -> 30% of each run, Pallas kernels for 0% -> 5%
where the time goes in v1:
time: 744 us; the launch traced here: 736 us
  waiting for transfers between devices  215 us (29%)
  local copies, waits for them, and re-layouts  189 us (25%)
  Pallas kernels  96.2 us (13%)
  matrix products  87.1 us (12%)
  other arithmetic  57.1 us (8%)
  blocking collectives  40.2 us (5%)
  starting transfers between devices  31.7 us (4%)
  between operations  19.1 us (3%)
    ppermute x28, waiting for transfers between devices, hop(): return lax.ppermute(x, axis, [(i, i ^ k) for i in range(n)])  109 us
    dot_general x25, matrix products, mm(): lax.dot_general(a, b, ((ca, cb), ((), ())), preferred_element_type=f32)  85.9 us
    all_gather x1, waiting for transfers between devices, per_device(): first_all = lax.all_gather(first, ('samp', 'tok'), axis=0)  71.9 us
    unnamed x191, local copies, waits for them, and re-layouts  61.6 us
    psum x1, blocking collectives, per_device(): lax.psum((noise_part, pairhead_part), ('samp', 'tok'))  40.2 us
    pallas_call x1, Pallas kernels, pair_bwd(): pl.pallas_call(_pair_bwd, grid=(R // blk,), in_specs=[pl.BlockSpec((blk,...  35.7 us
    all_gather x1, waiting for transfers between devices, per_device(): second_all = lax.all_gather(second, ('samp', 'tok'), axis=0)  34.2 us
    ppermute x28, starting transfers between devices, hop(): return lax.ppermute(x, axis, [(i, i ^ k) for i in range(n)])  31.5 us
  transfers between devices with their start and end apart: 32, of which 12 were waited for; matrix products, arithmetic and copies ran while one was open for 30% of the time, Pallas kernels for 5%

profile of v1, /device:TPU:0, one launch (start us, length us, event | category | flops | bytes accessed | tf_op | source)
XLA Modules:
  0.0 735.9 jit_solution(3598747851101034460)
XLA Ops:
  7.3 11.9 %pair_bias.1 = bf16[16,192,96]{2,1,0:T(8,128)(2,1)} custom-call(bf16[192,96,128]{2,1,0:T(8,128)(2,1)} %bitcast.281, bf16[16,128]{1,0:T(8,128)(2,1)} %bitcast.344), custom_call_target="tpu_custom_call" | custom-call | flops 75497472 | bytes 4718592 | tf_op jit(solution)/shard_map/pair_bias/pallas_call | solution.py:98
  21.3 4.1 collective-permute-start.1
  39.2 18.9 %collective-permute-done = bf16[480,768]{1,0:T(8,128)(2,1)} collective-permute-done((bf16[480,768]{1,0:T(8,128)(2,1)S(1)}, bf16[480,768]{1,0:T(8,128)(2,1)}, u32[]{:S(2)}, u32[]{:S(2)}) %collective-permute-start) | collective-permute-done | bytes 737312 | tf_op jit(solution)/shard_map/ppermute | solution.py:164
  62.2 12.6 %collective-permute-done.2 = bf16[480,768]{1,0:T(8,128)(2,1)} collective-permute-done((bf16[480,768]{1,0:T(8,128)(2,1)S(1)}, bf16[480,768]{1,0:T(8,128)(2,1)}, u32[]{:S(2)}, u32[]{:S(2)}) %collective-permute-start.2) | collective-permute-done | bytes 737312 | tf_op jit(solution)/shard_map/ppermute | solution.py:164
  82.8 2.5 copy.335
  85.3 6.5 copy.337
  92.9 10.8 %copy.446 = bf16[8,16,192,96]{3,0,2,1:T(8,128)(2,1)} copy(bf16[8,16,192,96]{3,2,1,0:T(8,128)(2,1)} %bitcast.300) | data formatting | bytes 9437184 | tf_op jit(solution)/shard_map/all_gather | solution.py:264
  103.6 11.0 %reshape.424.bias_ref = bf16[16,192,768]{2,1,0:T(8,128)(2,1)} reshape(bf16[16,192,8,96]{3,2,1,0:T(8,128)(2,1)} %bitcast.279) | data formatting | bytes 9437184 | tf_op jit(solution)/shard_map/reshape | solution.py:264
  114.6 34.2 %all-gather.11.cloned.1.call-done = bf16[5376,768]{1,0:T(8,128)(2,1)} async-done(((bf16[168,768]{1,0:T(8,128)(2,1)}), bf16[5376,768]{1,0:T(8,128)(2,1)}) %all-gather.11.cloned.1.call-update) | async-done | bytes 8257552 | tf_op jit(solution)/shard_map/all_gather | solution.py:244
  148.8 3.3 slice.356
  152.1 5.4 fusion.120
  157.5 71.9 %all-gather.7.cloned.1.call-done = bf16[5632,768]{1,0:T(8,128)(2,1)} async-done(((bf16[176,768]{1,0:T(8,128)(2,1)}), bf16[5632,768]{1,0:T(8,128)(2,1)}) %all-gather.7.cloned.1.call-update) | async-done | bytes 8650768 | tf_op jit(solution)/shard_map/all_gather | solution.py:243
  230.6 3.6 fusion.119
  234.2 4.6 fusion.118
  241.3 2.9 convolution_add_fusion
  244.8 3.0 fusion.117
  250.0 3.2 convolution_negate_fusion
  255.0 5.7 convolution_convert_fusion.v_ref
  260.7 3.6 convolution_convert_fusion.1.k_ref
  264.3 24.5 %attention.1 = (bf16[16,2,192,768]{3,2,1,0:T(8,128)(2,1)}, f32[2,192,768]{2,1,0:T(8,128)}) custom-call(bf16[2,192,768]{2,1,0:T(8,128)(2,1)} %copy.348.q_ref, bf16[2,768,768]{2,1,0:T(8,128)(2,1)} %convolution_convert_fusion.1.k_ref, bf16[2,768,768]{2,1,0:T(8,128)(2,1)} %convolution_convert_fusion.v_ref, bf16[16,192,768]{2,1,0:T(8,128)(2,1)} %reshape.424.bias_ref, ...), custom_call_target="tpu_custom_call" | custom-call | flops 4831838208 | bytes 20000000 | tf_op jit(solution)/shard_map/attention/pallas_call | solution.py:37
  288.8 2.9 copy.349
  291.7 3.7 convolution_add_fusion.1
  307.9 3.1 multiply_convert_fusion.1
  311.0 4.1 fusion.111
  319.2 2.2 bitcast_convert_fusion.2
  323.7 24.1 %attention_back.1 = (f32[2,192,768]{2,1,0:T(8,128)}, bf16[2,768,768]{2,1,0:T(8,128)(2,1)}, bf16[2,768,768]{2,1,0:T(8,128)(2,1)}, bf16[16,192,768]{2,1,0:T(8,128)(2,1)}) custom-call(bf16[16,2,192,768]{3,2,1,0:T(8,128)(2,1)} %get-tuple-element.47.p_ref, bf16[2,192,768]{2,1,0:T(8,128)(2,1)} %copy.362.do_ref, ...), custom_call_target="tpu_custom_call" | custom-call | flops 9663676416 | bytes 30000000 | tf_op jit(solution)/shard_map/attention_back/pallas_call | solution.py:70
  347.7 4.9 bitcast_convert_fusion.5
  352.6 4.3 fusion.132
  356.9 4.7 bitcast_convert_fusion
  367.1 5.6 bitcast_convert_fusion.4
  372.7 4.4 add_convert_fusion
  378.6 2.3 copy.430
  385.2 11.5 %reshape.434 = bf16[3072,8,96]{2,1,0:T(8,128)(2,1)} reshape(bf16[16,192,768]{2,1,0:T(8,128)(2,1)} %get-tuple-element.51) | data formatting | bytes 9437184 | tf_op jit(solution)/shard_map/reshape | solution.py:351
  396.7 4.8 fusion.121
  401.6 2.8 bitcast_convert_fusion.1
  404.4 14.2 %constant_dynamic-slice_fusion.1 = (bf16[4,1,3072,96]{3,1,0,2:T(2,128)(2,1)}, bf16[4,1,3072,96]{3,1,0,2:T(2,128)(2,1)}) fusion(bf16[4,2,3072,96]{3,1,0,2:T(2,128)(2,1)S(1)} %bitcast.275, s32[]{:T(128)S(6)} %select_n.110, s32[]{:T(128)S(6)} %select_n.111), kind=kLoop, calls=%fused_computation.231 | loop fusion | bytes 9437192 | tf_op jit(solution)/shard_map/jit(dynamic_index_in_dim)/dynamic_slice | solution.py:204
  418.7 13.7 %copy.432 = bf16[4,1,3072,96]{2,3,1,0:T(8,128)(2,1)} copy(bf16[4,1,3072,96]{3,1,0,2:T(2,128)(2,1)} %get-tuple-element.172) | data formatting | bytes 4718592
  432.5 2.5 constant_dynamic-update-slice_fusion.16
  439.7 2.3 dynamic-slice_bitcast_fusion.1
  454.7 2.2 copy.367
  456.9 2.3 copy.366
  459.2 5.6 fusion.23
  464.8 3.7 fusion.110
  468.6 4.1 fusion.25
  476.8 3.2 fusion.29
  480.0 4.4 reduce_sum.198
  484.9 6.2 fusion.2
  494.4 4.6 dynamic-slice_bitcast_fusion
  499.7 6.0 fusion.112
  509.1 12.4 %copy.431 = bf16[4,1,3072,96]{2,3,0,1:T(8,128)(2,1)S(1)} copy(bf16[4,1,3072,96]{3,1,0,2:T(2,128)(2,1)} %get-tuple-element.171) | data formatting | bytes 4718592
  525.9 2.9 copy.398
  529.4 4.4 fusion.1
  537.6 2.6 fusion.4
  541.8 18.7 %collective-permute-done.22 = bf16[672,768]{1,0:T(8,128)(2,1)S(1)} collective-permute-done((bf16[672,768]{1,0:T(8,128)(2,1)S(1)}, bf16[672,768]{1,0:T(8,128)(2,1)S(1)}, u32[]{:S(2)}, u32[]{:S(2)}) %collective-permute-start.22) | collective-permute-done | bytes 1032224 | tf_op jit(solution)/shard_map/ppermute | solution.py:164
  561.9 21.7 %collective-permute-done.24 = bf16[672,768]{1,0:T(8,128)(2,1)S(1)} collective-permute-done((bf16[672,768]{1,0:T(8,128)(2,1)S(1)}, bf16[672,768]{1,0:T(8,128)(2,1)S(1)}, u32[]{:S(2)}, u32[]{:S(2)}) %collective-permute-start.24) | collective-permute-done | bytes 1032224 | tf_op jit(solution)/shard_map/ppermute | solution.py:164
  586.0 4.6 fusion
  596.8 12.3 %collective-permute-done.13 = bf16[3072,96]{0,1:T(8,128)(2,1)S(1)} collective-permute-done((bf16[3072,96]{0,1:T(8,128)(2,1)S(1)}, bf16[3072,96]{0,1:T(8,128)(2,1)S(1)}, u32[]{:S(2)}, u32[]{:S(2)}) %collective-permute-start.13) | collective-permute-done | bytes 589856 | tf_op jit(solution)/shard_map/ppermute | solution.py:164
  612.8 2.5 copy.383
  615.3 35.7 %pair_back.1 = (f32[192,96,128]{2,1,0:T(8,128)}, f32[16,128]{1,0:T(8,128)}) custom-call(bf16[192,96,128]{2,1,0:T(8,128)(2,1)} %bitcast.282, f32[192,16,96]{2,1,0:T(8,128)} %bitcast.301, bf16[16,128]{1,0:T(8,128)(2,1)} %bitcast.345), custom_call_target="tpu_custom_call" | custom-call | flops 301989888 | bytes 14155776 | tf_op jit(solution)/shard_map/pair_back/pallas_call | solution.py:134
  651.0 40.2 %psum.15 = f32[128,16]{0,1:T(8,128)} all-reduce(f32[128,16]{0,1:T(8,128)} %bitcast.346), channel_id=1, replica_groups=mesh['samp'=8,'tok'=4] {'samp','tok'}, use_global_device_ids=true, to_apply=%region_21.22 | all-reduce | flops 2048 | bytes 16384 | tf_op jit(solution)/shard_map/psum | solution.py:394
  694.0 2.7 fusion.15
  701.1 5.9 collective-permute-done.18
  707.0 5.4 collective-permute-done.20
  712.4 11.7 %collective-permute-done.19 = bf16[176,768]{1,0:T(8,128)(2,1)S(1)} collective-permute-done((bf16[176,768]{1,0:T(8,128)(2,1)S(1)}, bf16[176,768]{1,0:T(8,128)(2,1)S(1)}, u32[]{:S(2)}, u32[]{:S(2)}) %collective-permute-start.19) | collective-permute-done | bytes 270368 | tf_op jit(solution)/shard_map/ppermute | solution.py:164
  (369 shorter events, 128.5 us)
Async XLA Ops:
  7.2 85.7 %all-gather.9.cloned.1.call-start = ((), (), s32[]{:S(2)}) async-start(), calls=%async_computation.2 | async-start | bytes 7077888 | tf_op jit(solution)/shard_map/all_gather | solution.py:264
  7.2 12.1 %copy-start.55 = (bf16[24,3072]{1,0:T(8,128)(2,1)S(1)}, bf16[24,3072]{1,0:T(8,128)(2,1)}, u32[]{:S(2)}) copy-start(bf16[24,3072]{1,0:T(8,128)(2,1)} %param.33) | copy-start | bytes 442372
  7.2 12.1 %copy-start.59 = (bf16[24,768]{1,0:T(8,128)(2,1)S(1)}, bf16[24,768]{1,0:T(8,128)(2,1)}, u32[]{:S(2)}) copy-start(bf16[24,768]{1,0:T(8,128)(2,1)} %param.32) | copy-start | bytes 110596
  7.2 12.1 %copy-start.58 = (bf16[48,768]{1,0:T(8,128)(2,1)S(1)}, bf16[48,768]{1,0:T(8,128)(2,1)}, u32[]{:S(2)}) copy-start(bf16[48,768]{1,0:T(8,128)(2,1)} %param.34) | copy-start | bytes 221188
  7.3 12.9 %copy-start.63 = (bf16[24]{0:T(256)(128)(2,1)S(1)}, bf16[24]{0:T(256)(128)(2,1)}, u32[]{:S(2)}) copy-start(bf16[24]{0:T(256)(128)(2,1)} %param.31) | copy-start | bytes 148
  7.3 12.9 %copy-start.64 = (bf16[48]{0:T(256)(128)(2,1)S(1)}, bf16[48]{0:T(256)(128)(2,1)}, u32[]{:S(2)}) copy-start(bf16[48]{0:T(256)(128)(2,1)} %param.29) | copy-start | bytes 292
  7.3 12.9 %copy-start.65 = (bf16[96]{0:T(256)(128)(2,1)S(1)}, bf16[96]{0:T(256)(128)(2,1)}, u32[]{:S(2)}) copy-start(bf16[96]{0:T(256)(128)(2,1)} %param.28) | copy-start | bytes 580
  7.3 13.0 %copy-start.56 = (bf16[24,3072]{1,0:T(8,128)(2,1)S(1)}, bf16[24,3072]{1,0:T(8,128)(2,1)}, u32[]{:S(2)}) copy-start(bf16[24,3072]{1,0:T(8,128)(2,1)} %param.30) | copy-start | bytes 442372
  19.2 129.6 %all-gather.11.cloned.1.call-start = ((), (), s32[]{:S(2)}) async-start(), calls=%async_computation.3 | async-start | bytes 8515584 | tf_op jit(solution)/shard_map/all_gather | solution.py:244
  19.3 7.7 %copy-start.60 = (s32[2]{0:T(128)S(1)}, s32[2]{0:T(128)}, u32[]{:S(2)}) copy-start(s32[2]{0:T(128)} %param.24) | copy-start | bytes 28
  20.1 209.2 %all-gather.7.cloned.1.call-start = ((), (), s32[]{:S(2)}) async-start(), calls=%async_computation.1 | async-start | bytes 8921088 | tf_op jit(solution)/shard_map/all_gather | solution.py:243
  21.1 706.3 %all-reduce.4.cloned.1.call-start = ((), (), s32[]{:S(2)}) async-start(), calls=%async_computation | async-start | bytes 786432 | tf_op jit(solution)/shard_map/psum | solution.py:394
  21.3 38.9 %collective-permute-start.1 = (bf16[480,768]{1,0:T(8,128)(2,1)S(1)}, bf16[480,768]{1,0:T(8,128)(2,1)}, u32[]{:S(2)}, u32[]{:S(2)}) collective-permute-start(bf16[480,768]{1,0:T(8,128)(2,1)S(1)} %maximum_maximum_fusion), channel_id=1, source_target_pairs={{0,2},{1,3},{2,0},{3,1},{4,6},{5,7},{6,4},{7,5},{8,10},{9,11},{10,... | collective-permute-start | bytes 2211848 | tf_op jit(solution)/shard_map/ppermute | solution.py:164
  25.4 32.7 %collective-permute-start = (bf16[480,768]{1,0:T(8,128)(2,1)S(1)}, bf16[480,768]{1,0:T(8,128)(2,1)}, u32[]{:S(2)}, u32[]{:S(2)}) collective-permute-start(bf16[480,768]{1,0:T(8,128)(2,1)S(1)} %maximum_maximum_fusion), channel_id=1, source_target_pairs={{0,1},{1,0},{2,3},{3,2},{4,5},{5,4},{6,7},{7,6},{8,9},{9,8},{10,11... | collective-permute-start | bytes 2211848 | tf_op jit(solution)/shard_map/ppermute | solution.py:164
  27.0 47.8 %collective-permute-start.2 = (bf16[480,768]{1,0:T(8,128)(2,1)S(1)}, bf16[480,768]{1,0:T(8,128)(2,1)}, u32[]{:S(2)}, u32[]{:S(2)}) collective-permute-start(bf16[480,768]{1,0:T(8,128)(2,1)S(1)} %maximum_maximum_fusion), channel_id=1, source_target_pairs={{0,3},{1,2},{2,1},{3,0},{4,7},{5,6},{6,5},{7,4},{8,11},{9,10},{10,... | collective-permute-start | bytes 2211848 | tf_op jit(solution)/shard_map/ppermute | solution.py:164
  85.3 6.5 copy-start.8
  239.4 4.8 slice-start.2
  255.0 40.4 %copy-start.12 = (f32[2,192,768]{1,2,0:T(8,128)}, f32[2,192,768]{1,2,0:T(8,128)S(1)}, u32[]{:S(2)}) copy-start(f32[2,192,768]{1,2,0:T(8,128)S(1)} %copy.341) | copy-start | bytes 3538948
  255.0 5.7 copy-start.28
  255.0 5.7 copy-start.35
  295.4 19.7 %copy-start.2 = (f32[2,192,3072]{1,2,0:T(8,128)}, f32[2,192,3072]{1,2,0:T(8,128)S(1)}, u32[]{:S(2)}) copy-start(f32[2,192,3072]{1,2,0:T(8,128)S(1)} %convolution_add_fusion.1) | copy-start | bytes 14155780
  323.6 24.1 %copy-start.29 = (bf16[2,768,768]{1,2,0:T(8,128)(2,1)S(1)}, bf16[2,768,768]{1,2,0:T(8,128)(2,1)}, u32[]{:S(2)}) copy-start(bf16[2,768,768]{1,2,0:T(8,128)(2,1)} %copy-done.27) | copy-start | bytes 7077892
  347.7 4.9 copy-start.36
  347.7 4.9 copy-start.69
  352.6 4.3 copy-start.49
  352.6 4.3 copy-start.73
  352.6 4.3 copy-start.75
  356.9 4.7 copy-start.66
  367.0 5.6 copy-start.33
  367.1 5.6 copy-start.68
  380.8 71.7 %collective-permute-start.5 = (bf16[2,192,768]{2,1,0:T(8,128)(2,1)}, bf16[2,192,768]{2,1,0:T(8,128)(2,1)}, u32[]{:S(2)}, u32[]{:S(2)}) collective-permute-start(bf16[2,192,768]{2,1,0:T(8,128)(2,1)} %get-tuple-element.196), channel_id=1, source_target_pairs={{0,3},{1,2},{2,1},{3,0},{4,7},{5,6},{6,5},{7,4},{8,11},{9,10},{10,... | collective-permute-start | bytes 1769480 | tf_op jit(solution)/shard_map/ppermute | solution.py:164
  382.7 72.0 %collective-permute-start.4 = (bf16[2,192,768]{2,1,0:T(8,128)(2,1)}, bf16[2,192,768]{2,1,0:T(8,128)(2,1)}, u32[]{:S(2)}, u32[]{:S(2)}) collective-permute-start(bf16[2,192,768]{2,1,0:T(8,128)(2,1)} %get-tuple-element.197), channel_id=1, source_target_pairs={{0,2},{1,3},{2,0},{3,1},{4,6},{5,7},{6,4},{7,5},{8,10},{9,11},{10,... | collective-permute-start | bytes 1769480 | tf_op jit(solution)/shard_map/ppermute | solution.py:164
  383.8 73.2 %collective-permute-start.3 = (bf16[2,192,768]{2,1,0:T(8,128)(2,1)}, bf16[2,192,768]{2,1,0:T(8,128)(2,1)}, u32[]{:S(2)}, u32[]{:S(2)}) collective-permute-start(bf16[2,192,768]{2,1,0:T(8,128)(2,1)} %get-tuple-element.198), channel_id=1, source_target_pairs={{0,1},{1,0},{2,3},{3,2},{4,5},{5,4},{6,7},{7,6},{8,9},{9,8},{10,11... | collective-permute-start | bytes 1769480 | tf_op jit(solution)/shard_map/ppermute | solution.py:164
  396.7 4.9 copy-start.47
  396.7 4.9 copy-start.70
  396.7 7.7 %slice-start = ((s8[6291456]{0:T(1024)(128)(4,1)}), s8[2097152]{0:T(1024)(128)(4,1)S(1)}, s32[]{:S(2)}) async-start(s8[6291456]{0:T(1024)(128)(4,1)} %bitcast.273), calls=%async_computation.4 | async-start | bytes 4194304
  432.4 105.2 %collective-permute-start.10 = (bf16[4,3072,96]{1,2,0:T(8,128)(2,1)}, bf16[4,3072,96]{1,2,0:T(8,128)(2,1)}, u32[]{:S(2)}, u32[]{:S(2)}) collective-permute-start(bf16[4,3072,96]{1,2,0:T(8,128)(2,1)} %bitcast.317), channel_id=1, source_target_pairs={{0,4},{4,0},{8,12},{12,8},{16,20},{20,16},{24,28},{28,24},{1,5},{5... | collective-permute-start | bytes 7077896 | tf_op jit(solution)/shard_map/ppermute | solution.py:164
  439.7 4.4 copy-start.7
  439.7 4.8 copy-start.42
  444.1 85.3 %collective-permute-start.21 = (bf16[4,672,768]{2,1,0:T(8,128)(2,1)}, bf16[4,672,768]{2,1,0:T(8,128)(2,1)}, u32[]{:S(2)}, u32[]{:S(2)}) collective-permute-start(bf16[4,672,768]{2,1,0:T(8,128)(2,1)} %dynamic-slice_bitcast_fusion.1), channel_id=1, source_target_pairs={{0,4},{4,0},{8,12},{12,8},{16,20},{20,16},{24,28},{28,24},{1,5},{5... | collective-permute-start | bytes 12386312 | tf_op jit(solution)/shard_map/ppermute | solution.py:164
  464.8 7.8 %slice-start.4 = ((s8[6291456]{0:T(1024)(128)(4,1)}), s8[4194304]{0:T(1024)(128)(4,1)S(1)}, s32[]{:S(2)}) async-start(s8[6291456]{0:T(1024)(128)(4,1)} %bitcast.286), calls=%async_computation.8 | async-start | bytes 8388608
  494.4 5.4 copy-start.4
  499.0 87.0 %collective-permute-start.14 = (bf16[4,704,768]{2,1,0:T(8,128)(2,1)}, bf16[4,704,768]{2,1,0:T(8,128)(2,1)}, u32[]{:S(2)}, u32[]{:S(2)}) collective-permute-start(bf16[4,704,768]{2,1,0:T(8,128)(2,1)} %dynamic-slice_bitcast_fusion), channel_id=1, source_target_pairs={{0,4},{4,0},{8,12},{12,8},{16,20},{20,16},{24,28},{28,24},{1,5},{5... | collective-permute-start | bytes 12976136 | tf_op jit(solution)/shard_map/ppermute | solution.py:164
  506.2 1.4 collective-permute-start.6
  507.6 15.4 %collective-permute-start.7 = (bf16[48,192]{1,0:T(8,128)(2,1)S(1)}, bf16[48,192]{1,0:T(8,128)(2,1)S(1)}, u32[]{:S(2)}, u32[]{:S(2)}) collective-permute-start(bf16[48,192]{1,0:T(8,128)(2,1)S(1)} %get-tuple-element.226), channel_id=1, source_target_pairs={{0,8},{4,12},{8,0},{12,4},{16,24},{20,28},{24,16},{28,20},{1,9},{5... | collective-permute-start | bytes 55304 | tf_op jit(solution)/shard_map/ppermute | solution.py:164
  509.1 14.5 %copy-start.61 = (s32[2]{0:T(128)S(1)}, s32[2]{0:T(128)}, u32[]{:S(2)}) copy-start(s32[2]{0:T(128)} %param.24) | copy-start | bytes 28
  509.1 15.7 %copy-start.50 = (bf16[2,192,768]{1,2,0:T(8,128)(2,1)S(1)}, bf16[2,192,768]{1,2,0:T(8,128)(2,1)}, u32[]{:S(2)}) copy-start(bf16[2,192,768]{1,2,0:T(8,128)(2,1)} %get-tuple-element.168) | copy-start | bytes 1769476
  521.5 7.3 collective-permute-start.9
  523.0 5.8 collective-permute-start.8
  534.1 26.4 %collective-permute-start.22 = (bf16[672,768]{1,0:T(8,128)(2,1)S(1)}, bf16[672,768]{1,0:T(8,128)(2,1)S(1)}, u32[]{:S(2)}, u32[]{:S(2)}) collective-permute-start(bf16[672,768]{1,0:T(8,128)(2,1)S(1)} %get-tuple-element.183), channel_id=1, source_target_pairs={{0,8},{4,12},{8,0},{12,4},{16,24},{20,28},{24,16},{28,20},{1,9},{5... | collective-permute-start | bytes 3096584 | tf_op jit(solution)/shard_map/ppermute | solution.py:164
  535.6 48.0 %collective-permute-start.24 = (bf16[672,768]{1,0:T(8,128)(2,1)S(1)}, bf16[672,768]{1,0:T(8,128)(2,1)S(1)}, u32[]{:S(2)}, u32[]{:S(2)}) collective-permute-start(bf16[672,768]{1,0:T(8,128)(2,1)S(1)} %get-tuple-element.184), channel_id=1, source_target_pairs={{0,24},{4,28},{8,16},{12,20},{16,8},{20,12},{24,0},{28,4},{1,25},{... | collective-permute-start | bytes 3096584 | tf_op jit(solution)/shard_map/ppermute | solution.py:164
  537.1 47.0 %collective-permute-start.23 = (bf16[672,768]{1,0:T(8,128)(2,1)S(1)}, bf16[672,768]{1,0:T(8,128)(2,1)S(1)}, u32[]{:S(2)}, u32[]{:S(2)}) collective-permute-start(bf16[672,768]{1,0:T(8,128)(2,1)S(1)} %get-tuple-element.185), channel_id=1, source_target_pairs={{0,16},{4,20},{8,24},{12,28},{16,0},{20,4},{24,8},{28,12},{1,17},{... | collective-permute-start | bytes 3096584 | tf_op jit(solution)/shard_map/ppermute | solution.py:164
  540.3 55.2 %collective-permute-start.11 = (bf16[3072,96]{0,1:T(8,128)(2,1)S(1)}, bf16[3072,96]{0,1:T(8,128)(2,1)S(1)}, u32[]{:S(2)}, u32[]{:S(2)}) collective-permute-start(bf16[3072,96]{0,1:T(8,128)(2,1)S(1)} %get-tuple-element.192), channel_id=1, source_target_pairs={{0,8},{4,12},{8,0},{12,4},{16,24},{20,28},{24,16},{28,20},{1,9},{5... | collective-permute-start | bytes 1769480 | tf_op jit(solution)/shard_map/ppermute | solution.py:164
  560.5 48.6 %collective-permute-start.13 = (bf16[3072,96]{0,1:T(8,128)(2,1)S(1)}, bf16[3072,96]{0,1:T(8,128)(2,1)S(1)}, u32[]{:S(2)}, u32[]{:S(2)}) collective-permute-start(bf16[3072,96]{0,1:T(8,128)(2,1)S(1)} %get-tuple-element.193), channel_id=1, source_target_pairs={{0,24},{4,28},{8,16},{12,20},{16,8},{20,12},{24,0},{28,4},{1,25},{... | collective-permute-start | bytes 1769480 | tf_op jit(solution)/shard_map/ppermute | solution.py:164
  583.6 26.0 %collective-permute-start.12 = (bf16[3072,96]{0,1:T(8,128)(2,1)S(1)}, bf16[3072,96]{0,1:T(8,128)(2,1)S(1)}, u32[]{:S(2)}, u32[]{:S(2)}) collective-permute-start(bf16[3072,96]{0,1:T(8,128)(2,1)S(1)} %get-tuple-element.194), channel_id=1, source_target_pairs={{0,16},{4,20},{8,24},{12,28},{16,0},{20,4},{24,8},{28,12},{1,17},{... | collective-permute-start | bytes 1769480 | tf_op jit(solution)/shard_map/ppermute | solution.py:164
  584.7 26.4 %collective-permute-start.25 = (bf16[168,768]{1,0:T(8,128)(2,1)S(1)}, bf16[168,768]{1,0:T(8,128)(2,1)S(1)}, u32[]{:S(2)}, u32[]{:S(2)}) collective-permute-start(bf16[168,768]{1,0:T(8,128)(2,1)S(1)} %get-tuple-element.202), channel_id=1, source_target_pairs={{0,1},{1,0},{2,3},{3,2},{4,5},{5,4},{6,7},{7,6},{8,9},{9,8},{10,11... | collective-permute-start | bytes 774152 | tf_op jit(solution)/shard_map/ppermute | solution.py:164
  593.6 100.3 %collective-permute-start.15 = (bf16[704,768]{1,0:T(8,128)(2,1)}, bf16[704,768]{1,0:T(8,128)(2,1)}, u32[]{:S(2)}, u32[]{:S(2)}) collective-permute-start(bf16[704,768]{1,0:T(8,128)(2,1)} %get-tuple-element.180), channel_id=1, source_target_pairs={{0,8},{4,12},{8,0},{12,4},{16,24},{20,28},{24,16},{28,20},{1,9},{5... | collective-permute-start | bytes 3244040 | tf_op jit(solution)/shard_map/ppermute | solution.py:164
  595.5 98.5 %collective-permute-start.17 = (bf16[704,768]{1,0:T(8,128)(2,1)}, bf16[704,768]{1,0:T(8,128)(2,1)}, u32[]{:S(2)}, u32[]{:S(2)}) collective-permute-start(bf16[704,768]{1,0:T(8,128)(2,1)} %get-tuple-element.181), channel_id=1, source_target_pairs={{0,24},{4,28},{8,16},{12,20},{16,8},{20,12},{24,0},{28,4},{1,25},{... | collective-permute-start | bytes 3244040 | tf_op jit(solution)/shard_map/ppermute | solution.py:164
  609.1 84.9 %collective-permute-start.16 = (bf16[704,768]{1,0:T(8,128)(2,1)}, bf16[704,768]{1,0:T(8,128)(2,1)}, u32[]{:S(2)}, u32[]{:S(2)}) collective-permute-start(bf16[704,768]{1,0:T(8,128)(2,1)} %get-tuple-element.182), channel_id=1, source_target_pairs={{0,16},{4,20},{8,24},{12,28},{16,0},{20,4},{24,8},{28,12},{1,17},{... | collective-permute-start | bytes 3244040 | tf_op jit(solution)/shard_map/ppermute | solution.py:164
  609.6 81.6 %collective-permute-start.27 = (bf16[168,768]{1,0:T(8,128)(2,1)S(1)}, bf16[168,768]{1,0:T(8,128)(2,1)}, u32[]{:S(2)}, u32[]{:S(2)}) collective-permute-start(bf16[168,768]{1,0:T(8,128)(2,1)S(1)} %get-tuple-element.203), channel_id=1, source_target_pairs={{0,3},{1,2},{2,1},{3,0},{4,7},{5,6},{6,5},{7,4},{8,11},{9,10},{10,... | collective-permute-start | bytes 774152 | tf_op jit(solution)/shard_map/ppermute | solution.py:164
  611.1 80.1 %collective-permute-start.26 = (bf16[168,768]{1,0:T(8,128)(2,1)S(1)}, bf16[168,768]{1,0:T(8,128)(2,1)}, u32[]{:S(2)}, u32[]{:S(2)}) collective-permute-start(bf16[168,768]{1,0:T(8,128)(2,1)S(1)} %get-tuple-element.204), channel_id=1, source_target_pairs={{0,2},{1,3},{2,0},{3,1},{4,6},{5,7},{6,4},{7,5},{8,10},{9,11},{10,... | collective-permute-start | bytes 774152 | tf_op jit(solution)/shard_map/ppermute | solution.py:164
  696.8 10.2 %collective-permute-start.18 = (bf16[176,768]{1,0:T(8,128)(2,1)S(1)}, bf16[176,768]{1,0:T(8,128)(2,1)S(1)}, u32[]{:S(2)}, u32[]{:S(2)}) collective-permute-start(bf16[176,768]{1,0:T(8,128)(2,1)S(1)} %get-tuple-element.199), channel_id=1, source_target_pairs={{0,1},{1,0},{2,3},{3,2},{4,5},{5,4},{6,7},{7,6},{8,9},{9,8},{10,11... | collective-permute-start | bytes 811016 | tf_op jit(solution)/shard_map/ppermute | solution.py:164
  696.9 15.5 %collective-permute-start.20 = (bf16[176,768]{1,0:T(8,128)(2,1)S(1)}, bf16[176,768]{1,0:T(8,128)(2,1)S(1)}, u32[]{:S(2)}, u32[]{:S(2)}) collective-permute-start(bf16[176,768]{1,0:T(8,128)(2,1)S(1)} %get-tuple-element.200), channel_id=1, source_target_pairs={{0,3},{1,2},{2,1},{3,0},{4,7},{5,6},{6,5},{7,4},{8,11},{9,10},{10,... | collective-permute-start | bytes 811016 | tf_op jit(solution)/shard_map/ppermute | solution.py:164
  698.6 25.5 %collective-permute-start.19 = (bf16[176,768]{1,0:T(8,128)(2,1)S(1)}, bf16[176,768]{1,0:T(8,128)(2,1)S(1)}, u32[]{:S(2)}, u32[]{:S(2)}) collective-permute-start(bf16[176,768]{1,0:T(8,128)(2,1)S(1)} %get-tuple-element.201), channel_id=1, source_target_pairs={{0,2},{1,3},{2,0},{3,1},{4,6},{5,7},{6,4},{7,5},{8,10},{9,11},{10,... | collective-permute-start | bytes 811016 | tf_op jit(solution)/shard_map/ppermute | solution.py:164
  (50 other events, 118.0 us)
Sparse Core Ops, SparseCore 0:
  19.4 48.2 all-gather.8
  71.0 77.7 all-gather.10
  152.2 77.1 all-gather.6
  526.0 185.8 all-reduce.3

commit v2 on v1

v2 whole, which is shorter than its diff:
```python
import jax
import jax.numpy as jnp
from jax import lax
from jax.experimental import pallas as pl
from jax.experimental.pallas import tpu as pltpu
from jax.sharding import PartitionSpec as P

DH = 48
EPS = 1e-5
WIN = 256
VMEM_BYTES = 56 * 1024 * 1024
f32 = jnp.float32
bf16 = jnp.bfloat16
COST = pl.CostEstimate(flops=1024, bytes_accessed=1024, transcendentals=0)
NT = (((1,), (1,)), ((), ()))
TN = (((0,), (0,)), ((), ()))


def params():
    return pltpu.CompilerParams(vmem_limit_bytes=VMEM_BYTES)


def window(h, width):
    w = pl.multiple_of(jnp.minimum((h * DH) // 128 * 128, width - WIN), 128)
    lane = lax.broadcasted_iota(jnp.int32, (1, WIN), 1) + w
    return w, (lane >= h * DH) & (lane < h * DH + DH)


def attention_body(q_ref, k_ref, v_ref, bias_ref, mask_ref, p_ref, att_ref):
    samples, _, width = q_ref.shape
    w, inside = window(pl.program_id(0), width)
    bias = bias_ref[0].astype(f32) + mask_ref[...]
    for b in range(samples):
        q = jnp.where(inside, q_ref[b, :, pl.ds(w, WIN)], 0)
        s = lax.dot_general(q, k_ref[b, :, pl.ds(w, WIN)], NT, preferred_element_type=f32)
        s = s * (DH ** -0.5) + bias
        e = jnp.exp(s - jnp.max(s, axis=1, keepdims=True))
        p = (e * (1.0 / jnp.sum(e, axis=1, keepdims=True))).astype(bf16)
        p_ref[0, b] = p
        o = jnp.dot(p, v_ref[b, :, pl.ds(w, WIN)], preferred_element_type=f32)
        att_ref[b, :, pl.ds(w, WIN)] = jnp.where(inside, o, att_ref[b, :, pl.ds(w, WIN)])


def attention(q, kv, bias, mask):
    S, R, D = q.shape
    N, H = kv.shape[1], bias.shape[0]

    def whole(*shape):
        return pl.BlockSpec(shape, lambda h: (0,) * len(shape))

    return pl.pallas_call(
        attention_body,
        grid=(H,),
        in_specs=[
            whole(S, R, D),
            whole(S, N, D),
            pl.BlockSpec((S, N, D), lambda h: (0, 0, 1)),
            pl.BlockSpec((1, R, N), lambda h: (h, 0, 0)),
            whole(1, N),
        ],
        out_specs=[pl.BlockSpec((1, S, R, N), lambda h: (h, 0, 0, 0)), whole(S, R, D)],
        out_shape=[jax.ShapeDtypeStruct((H, S, R, N), bf16), jax.ShapeDtypeStruct((S, R, D), f32)],
        compiler_params=params(),
        cost_estimate=COST,
        name="attention",
    )(q, kv, kv, bias, mask)


def attention_back_body(fold, me_ref, p_ref, do_ref, k_ref, v_ref, q_ref, dq_ref, dkv_ref, *rest):
    *bb_refs, qt, dot_ = rest
    samples, rows, width = do_ref.shape
    h = pl.program_id(0)
    w, inside = window(h, width)

    @pl.when(h == 0)
    def _():
        for b in range(samples):
            qt[b] = q_ref[b].astype(f32).T.astype(bf16)
            dot_[b] = do_ref[b].astype(f32).T.astype(bf16)

    own = pl.ds(pl.multiple_of(h * DH, 16), DH)
    acc = None
    for b in range(samples):
        do = jnp.where(inside, do_ref[b, :, pl.ds(w, WIN)], 0)
        dp = lax.dot_general(do, v_ref[b, :, pl.ds(w, WIN)], NT, preferred_element_type=f32)
        p_low = p_ref[0, b]
        p = p_low.astype(f32)
        ds = p * (dp - jnp.sum(p * dp, axis=1, keepdims=True))
        acc = ds if acc is None else acc + ds
        low = ds.astype(bf16)
        dq = jnp.dot(low, k_ref[b, :, pl.ds(w, WIN)], preferred_element_type=f32) * (DH ** -0.5)
        dq_ref[b, :, pl.ds(w, WIN)] = jnp.where(inside, dq, dq_ref[b, :, pl.ds(w, WIN)])
        dk = jnp.dot(qt[b, own, :], low, preferred_element_type=f32) * (DH ** -0.5)
        dkv_ref[b, 0] = dk.astype(bf16)
        dkv_ref[b, 1] = jnp.dot(dot_[b, own, :], p_low, preferred_element_type=f32).astype(bf16)
    if fold == 1:
        bb_refs[0][0] = acc.astype(bf16)
    else:
        kept_ref, given_ref = bb_refs
        count, _, part, lanes = kept_ref.shape
        c = lanes // fold
        odd = me_ref[0] % 2 == 1

        def piece(s):
            return jnp.concatenate(
                [acc[i * part : (i + 1) * part, s * c : (s + 1) * c] for i in range(fold)], axis=1
            )

        for j in range(count):
            first, second = piece(2 * j), piece(2 * j + 1)
            kept_ref[j, 0] = jnp.where(odd, second, first).astype(bf16)
            given_ref[j, 0] = jnp.where(odd, first, second).astype(bf16)


def attention_back(me, p, do, kv, q, first, fold, groups):
    H, S, R, N = p.shape
    D = do.shape[2]

    def whole(*shape):
        return pl.BlockSpec(shape, lambda h, m: (0,) * len(shape))

    if fold == 1:
        bb_specs, bb_shapes = [pl.BlockSpec((1, R, N), lambda h, m: (h, 0, 0))], [(H, R, N)]
    else:
        tail = (R // fold, fold * (N // groups))
        bb_specs = [pl.BlockSpec((groups // 2, 1) + tail, lambda h, m: (0, h, 0, 0))] * 2
        bb_shapes = [(groups // 2, H) + tail] * 2

    def body(me_ref, p_ref, do_ref, k_ref, v_ref, q_ref, _, *refs):
        attention_back_body(fold, me_ref, p_ref, do_ref, k_ref, v_ref, q_ref, *refs)

    return pl.pallas_call(
        body,
        grid_spec=pltpu.PrefetchScalarGridSpec(
            num_scalar_prefetch=1,
            grid=(H,),
            in_specs=[
                pl.BlockSpec((1, S, R, N), lambda h, m: (h, 0, 0, 0)),
                whole(S, R, D),
                whole(S, N, D),
                pl.BlockSpec((S, N, D), lambda h, m: (0, 0, 1)),
                whole(S, R, D),
                pl.BlockSpec(memory_space=pl.ANY),
            ],
            out_specs=[whole(S, R, D), pl.BlockSpec((S, 2, DH, N), lambda h, m: (0, 0, h, 0))] + bb_specs,
            scratch_shapes=[pltpu.VMEM((S, D, R), bf16), pltpu.VMEM((S, D, R), bf16)],
        ),
        out_shape=[
            jax.ShapeDtypeStruct((S, R, D), f32),
            jax.ShapeDtypeStruct((S, 2, D, N), bf16),
        ]
        + [jax.ShapeDtypeStruct(shape, bf16) for shape in bb_shapes],
        compiler_params=params(),
        cost_estimate=COST,
        name="attention_back",
    )(me, p, do, kv, kv, q, first)


def normal_rows(x):
    c = x - jnp.mean(x, axis=-1, keepdims=True)
    r = lax.rsqrt(jnp.mean(c * c, axis=-1, keepdims=True) + EPS)
    return c * r, r


def split(x):
    hi = x.astype(bf16)
    return hi, (x - hi.astype(f32)).astype(bf16)


def lane_mean(x):
    ones = jnp.full((x.shape[1], x.shape[1]), 1.0, bf16)
    hi, lo = split(x)
    total = jnp.dot(hi, ones, preferred_element_type=f32) + jnp.dot(lo, ones, preferred_element_type=f32)
    return total * (1.0 / x.shape[1])


def pair_bias_body(x_ref, ph_ref, out_ref, buf):
    fold, n, C, E = x_ref.shape
    ph = ph_ref[...]
    for i in range(n):
        x = x_ref[:, i].reshape(fold * C, E) if fold > 1 else x_ref[0, i]
        nrm, _ = normal_rows(x.astype(f32))
        buf[:, i, :] = lax.dot_general(ph, nrm.astype(bf16), NT, preferred_element_type=f32)
    out_ref[...] = buf[...].astype(bf16)


def pair_bias(x, pht, fold):
    R, C, E = x.shape
    H = pht.shape[0]
    rows = R // fold
    blk = 16
    return pl.pallas_call(
        pair_bias_body,
        grid=(rows // blk,),
        in_specs=[
            pl.BlockSpec((fold, blk, C, E), lambda i: (0, i, 0, 0)), pl.BlockSpec((H, E), lambda i: (0, 0)),
        ],
        out_specs=pl.BlockSpec((H, blk, fold * C), lambda i: (0, i, 0)),
        out_shape=jax.ShapeDtypeStruct((H, rows, fold * C), bf16),
        scratch_shapes=[pltpu.VMEM((H, blk, fold * C), f32)],
        compiler_params=params(),
        cost_estimate=COST,
        name="pair_bias",
    )(x.reshape(fold, rows, C, E), pht)


def pair_back_body(x_ref, bb_ref, ph_ref, out_ref, dph_ref):
    fold, n, C, E = x_ref.shape
    H = ph_ref.shape[0]
    ph = ph_ref[...].astype(f32)
    ph_hi, ph_lo = split(ph - jnp.mean(ph, axis=-1, keepdims=True))
    ph4 = jnp.concatenate([ph_hi, ph_lo, ph_hi, ph_lo], axis=0)
    acc = jnp.zeros((2 * H, E), f32)
    for i in range(n):
        x = x_ref[:, i].reshape(fold * C, E) if fold > 1 else x_ref[0, i]
        ones = jnp.full((E, E), 1.0, bf16)
        c = x.astype(f32) - jnp.dot(x, ones, preferred_element_type=f32) * (1.0 / E)
        r = lax.rsqrt(lane_mean(c * c) + EPS)
        nrm = c * r
        hi, lo = split(bb_ref[i])
        g = lax.dot_general(
            jnp.concatenate([hi, hi, lo, lo], axis=0), ph4, TN, preferred_element_type=f32
        )
        grad = r * (g - nrm * jnp.mean(g * nrm, axis=-1, keepdims=True))
        if fold > 1:
            out_ref[:, i] = grad.reshape(fold, C, E)
        else:
            out_ref[0, i] = grad
        acc += jnp.dot(jnp.concatenate([hi, lo], axis=0), nrm.astype(bf16), preferred_element_type=f32)
    part = acc[:H] + acc[H:]

    @pl.when(pl.program_id(0) == 0)
    def _():
        dph_ref[...] = part

    @pl.when(pl.program_id(0) != 0)
    def _():
        dph_ref[...] += part


def pair_back(x, bb, pht, fold):
    R, C, E = x.shape
    H = pht.shape[0]
    rows = R // fold
    blk = 8
    grad, dph = pl.pallas_call(
        pair_back_body,
        grid=(rows // blk,),
        in_specs=[
            pl.BlockSpec((fold, blk, C, E), lambda i: (0, i, 0, 0)),
            pl.BlockSpec((blk, H, fold * C), lambda i: (i, 0, 0)),
            pl.BlockSpec((H, E), lambda i: (0, 0)),
        ],
        out_specs=[pl.BlockSpec((fold, blk, C, E), lambda i: (0, i, 0, 0)), pl.BlockSpec((H, E), lambda i: (0, 0))],
        out_shape=[jax.ShapeDtypeStruct((fold, rows, C, E), f32), jax.ShapeDtypeStruct((H, E), f32)],
        compiler_params=params(),
        cost_estimate=COST,
        name="pair_back",
    )(x.reshape(fold, rows, C, E), bb, pht)
    return grad.reshape(R, C, E), dph


def lay_bias_body(me_ref, *refs):
    pieces, (out_ref, slots, sems) = refs[:-3], refs[-3:]
    h = pl.program_id(0)
    part, lanes = slots.shape[2:]
    fold = out_ref.shape[1] // part
    c = lanes // fold

    @pl.when(h == 0)
    def _():
        copies = [
            pltpu.make_async_copy(p, slots.at[jnp.bitwise_xor(me_ref[0], k)], sems.at[k]) for k, p in enumerate(pieces)
        ]
        for copy in copies:
            copy.start()
        for copy in copies:
            copy.wait()

    laid = [slots[s, h].astype(f32) for s in range(len(pieces))]
    for i in range(fold):
        out_ref[0, i * part : (i + 1) * part, :] = jnp.concatenate(
            [p[:, i * c : (i + 1) * c] for p in laid], axis=1
        ).astype(bf16)


def lay_bias(me, pieces, rows):
    H, part, lanes = pieces[0].shape
    count = len(pieces)
    keys = count * lanes // (rows // part)
    return pl.pallas_call(
        lay_bias_body,
        grid_spec=pltpu.PrefetchScalarGridSpec(
            num_scalar_prefetch=1,
            grid=(H,),
            in_specs=[pl.BlockSpec(memory_space=pl.ANY)] * count,
            out_specs=pl.BlockSpec((1, rows, keys), lambda h, s: (h, 0, 0)),
            scratch_shapes=[pltpu.VMEM((count, H, part, lanes), bf16), pltpu.SemaphoreType.DMA((count,))],
        ),
        out_shape=jax.ShapeDtypeStruct((H, rows, keys), bf16),
        compiler_params=params(),
        cost_estimate=COST,
        name="lay_bias",
    )(me, *pieces)


def lay_vectors_body(counts, x_ref, out_ref):
    x = x_ref[...]
    D = out_ref.shape[1]
    row = start = 0
    for n in counts:
        per = D // n
        for i in range(x.shape[0] // per):
            pieces = [x[j : j + 1, start : start + n] for j in range(i * per, (i + 1) * per)]
            out_ref[row : row + 1, :] = jnp.concatenate(pieces, axis=1)
            row += 1
        start += n
    out_ref[row:, :] = jnp.zeros((out_ref.shape[0] - row, D), f32)


def lay_vectors(x, *counts):
    D = x.shape[1]

    def body(x_ref, out_ref):
        lay_vectors_body(counts, x_ref, out_ref)

    return pl.pallas_call(
        body,
        out_shape=jax.ShapeDtypeStruct((8, D), f32),
        compiler_params=params(),
        cost_estimate=COST,
        name="lay_vectors",
    )(x)


def norm_back(n, r, g):
    return r * (g - jnp.mean(g, axis=-1, keepdims=True) - n * jnp.mean(g * n, axis=-1, keepdims=True))


def slope(s):
    return s * (1.0 - s)


def mm(a, b, ca, cb, out=f32):
    return lax.dot_general(a, b, ((ca, cb), ((), ())), preferred_element_type=f32).astype(out)


def hop(x, axis, k):
    return lax.ppermute(x, axis, [(i, i ^ k) for i in range(lax.axis_size(axis))])


def at(x, i):
    return lax.dynamic_index_in_dim(x, i, 0, keepdims=False)


def everyone(x, *others):
    steps = [(axis, 1 << i) for axis in ("tok", "samp") for i in range((lax.axis_size(axis) - 1).bit_length())]
    for i, (axis, k) in enumerate(steps):
        x = x + hop(x, axis, k)
        if i == 0:
            x = x + zero(*others).astype(f32)
    return x


def zero(*others):
    corners = [lax.slice(o, (0,) * o.ndim, (1,) * o.ndim).reshape(()).astype(f32) for o in others]
    return sum((jnp.abs(c) > 1e30).astype(jnp.int32) for c in corners)


def gather_tok(x, *others):
    n, t = lax.axis_size("tok"), lax.axis_index("tok")
    up, down = [x], [x]
    for _ in range(1, n):
        up.append(lax.ppermute(up[-1], "tok", [(i, i + 1) for i in range(n - 1)]))
        down.append(lax.ppermute(down[-1], "tok", [(i + 1, i) for i in range(n - 1)]))
    place = t + n + (zero(*others) if others else 0)
    out = jnp.zeros((n,) + x.shape, x.dtype)
    out = lax.dynamic_update_slice_in_dim(out, x[None], place % n, 0)
    for k in range(1, n):
        got = jnp.where(t >= k, up[k], down[n - k])
        out = lax.dynamic_update_slice_in_dim(out, got[None], (place - k) % n, 0)
    return out


def lay_tok(x, *others):
    n, t = lax.axis_size("tok"), lax.axis_index("tok")
    came = [x if k == 0 else hop(x, "tok", k) for k in range(n)]
    out = jnp.zeros((n,) + x.shape, x.dtype)
    place = t + zero(*others)
    for k in range(n):
        out = lax.dynamic_update_slice_in_dim(out, came[k][None], place ^ k, 0)
    return out


def sum_tok(x, *others, dim=0):
    n, t = lax.axis_size("tok"), lax.axis_index("tok")

    def part(i):
        return lax.dynamic_index_in_dim(x, i, dim, keepdims=False)

    came = [hop(part(t ^ k).astype(bf16), "tok", k) for k in range(1, n)]
    total = part(t + (zero(*others) if others else 0)).astype(f32)
    for c in came:
        total = total + c.astype(f32)
    return total


def sum_samp_start(parts, *others):
    n = lax.axis_size("samp")
    if n != 8:
        return jnp.concatenate([p.astype(bf16) for p in parts], axis=-2)
    c = lax.axis_index("samp") % 2

    def half(which):
        picked = [
            lax.dynamic_index_in_dim(p.reshape((n // 2, 2) + p.shape[1:]), which, 1, keepdims=False) for p in parts
        ]
        return jnp.concatenate(picked, axis=-2) if len(picked) > 1 else picked[0]

    other = hop(half(1 - c).astype(bf16), "samp", 1)
    both = half(c + zero(*others)).astype(f32) + other.astype(f32)
    return both.astype(bf16)


def sum_samp_end(both):
    n = lax.axis_size("samp")
    if n != 8:
        return lax.psum_scatter(both, "samp", scatter_dimension=0, tiled=False).astype(f32)
    j = lax.axis_index("samp") // 2
    total = at(both, j).astype(f32)
    for k in range(1, n // 2):
        total = total + hop(at(both, j ^ k), "samp", 2 * k).astype(f32)
    return total


def sum_samp(parts):
    return sum_samp_end(sum_samp_start(parts))


def per_device(
    tokens_in, cotangent, singles, noise_table, noise_level, pad_mask, pairwise, conditioner,
    offsets, shifts, projector, querybias, combiner, expander, reducer, pairhead,
):
    S, R, D = tokens_in.shape
    C = pairwise.shape[2]
    N = pad_mask.shape[1]
    H = pairhead.shape[1]
    CS = conditioner.shape[0]
    T, G = lax.axis_size("tok"), lax.axis_size("samp")
    W = G * T
    t, me = lax.axis_index("tok"), lax.axis_index("samp")
    fold = 4 if G == 8 else 1

    def blocks(w):
        return [w[:, i * D : (i + 1) * D] for i in range(w.shape[1] // D)]

    def rows_of(buf, start, count):
        return buf[:, start : start + count].reshape(W * count, D)

    cond_t = conditioner.T
    cc, pr, rr = cond_t.shape[0], projector.shape[0], reducer.shape[0]
    no, ns = offsets.shape[0], shifts.shape[0]
    vec = jnp.concatenate([offsets, shifts, querybias])
    vec_row = jnp.zeros((8, D), bf16).at[0, : vec.shape[0]].set(vec)
    cond_rows = jnp.concatenate([cond_t[: cc // 2], cond_t[cc // 2 :]], axis=1)
    q_block, k_block, v_block, g_block = blocks(projector)
    mine = lax.dynamic_slice_in_dim(singles[0], me * (R // G), R // G, 0)
    if R % (2 * G) == 0:
        single = jnp.concatenate([mine[: R // G // 2], mine[R // G // 2 :]], axis=1)
    else:
        single = jnp.pad(mine, ((0, 0), (0, D - CS)))
    single_rows = single.shape[0]
    first = jnp.concatenate([q_block, g_block, k_block, v_block, cond_rows, vec_row, single], axis=0)
    second = jnp.concatenate(blocks(expander) + [combiner, reducer], axis=0)
    first_all = lax.all_gather(first, ("samp", "tok"), axis=0)

    pht = pairhead.T
    piece = pair_bias(pairwise[0], pht, fold)
    if fold > 1:
        even = [piece] + [hop(piece, "samp", k) for k in range(2, G, 2)]
        pieces = [p for e in even for p in (e, hop(e, "samp", 1))]
        bias_all = lay_bias(me.astype(jnp.int32)[None], pieces, R)
    else:
        bias_all = jnp.transpose(lax.all_gather(piece, "samp", axis=0), (1, 2, 0, 3)).reshape(H, R, N)
    mask_add = (pad_mask.astype(f32) - 1.0) * 1e9
    every = gather_tok(jnp.concatenate([tokens_in.reshape(S * R, D), second], axis=0), bias_all)
    second_mine = lax.dynamic_slice_in_dim(every, S * R + zero(first_all), second.shape[0], 1)
    second_all = lax.all_gather(second_mine, "samp", axis=0).reshape(W, second.shape[0], D)

    tokens_all = every[:, : S * R].reshape(T, S, R, D).transpose(1, 0, 2, 3).reshape(S * N, D)
    token_norm_all, _ = normal_rows(tokens_all.astype(f32))
    singles_all = first_all[:, -single_rows:].reshape(G, T, single_rows, D).transpose(1, 0, 2, 3)
    if single_rows * 2 == R // G:
        halves = [singles_all[:, :, :, :CS], singles_all[:, :, :, CS:]]
        singles_all = jnp.concatenate(halves, axis=2).reshape(N, CS)
    else:
        singles_all = singles_all[:, :, :, :CS].reshape(N, CS)
    noise_rows = jnp.stack([at(noise_table, noise_level[b]) for b in range(S)])
    cond_all, _ = normal_rows((singles_all.astype(f32)[None] + noise_rows[:, None]).reshape(S * N, CS))
    cond_low_all = cond_all.astype(bf16)
    cond_norm, cond_inv = normal_rows((singles.astype(f32) + noise_rows[:, None]).reshape(S * R, CS))
    cond_low = cond_norm.astype(bf16)
    tokens = tokens_in.reshape(S * R, D).astype(f32)

    def own(x):
        return lax.dynamic_slice_in_dim(x.reshape(S, N, x.shape[-1]), t * R, R, 1).reshape(S * R, x.shape[-1])

    proj_full = jnp.concatenate([rows_of(first_all, i * pr, pr) for i in range(4)], axis=1)
    def cond_rows_of(start, stop):
        a, b = start // cc, -(-stop // cc)
        part = first_all[a:b, 4 * pr : 4 * pr + cc // 2]
        part = jnp.concatenate([part[:, :, :CS], part[:, :, CS:]], axis=1).reshape((b - a) * cc, CS)
        return part[start - a * cc : stop - a * cc]

    cond_pre, cond_rest = cond_rows_of(0, 2 * D), cond_rows_of(2 * D, 6 * D)
    vecs = first_all[:, 4 * pr + cc // 2].astype(f32)
    if fold > 1:
        rows = lay_vectors(vecs, no, ns, pr)
        o, sh, querybias_full = [rows[i : i + 1] for i in range(4)], [rows[4:5], rows[5:6]], rows[6:7]
    else:
        o = jnp.split(vecs[:, :no].reshape(1, W * no), 4, axis=1)
        sh = jnp.split(vecs[:, no : no + ns].reshape(1, W * ns), 2, axis=1)
        querybias_full = vecs[:, no + ns : no + ns + pr].reshape(1, W * pr)

    adapt_pre = mm(cond_low_all, cond_pre, (1,), (1,)) + jnp.concatenate([o[0], sh[0]], axis=1)
    gain_all = jax.nn.sigmoid(adapt_pre[:, :D])
    pre_all = (gain_all * token_norm_all + adapt_pre[:, D:]).astype(bf16)
    pre = own(pre_all)
    kv = mm(pre_all, proj_full[:, 2 * D :], (1,), (0,), bf16).reshape(S, N, 2 * D)
    query = (mm(pre, proj_full[:, :D], (1,), (0,)) + querybias_full).astype(bf16).reshape(S, R, D)
    gating = jax.nn.sigmoid(mm(pre, proj_full[:, D : 2 * D], (1,), (0,)))

    probs, attended = attention(query, kv, bias_all, mask_add)
    attended = attended.reshape(S * R, D)

    adapt_own = mm(cond_low, cond_rest, (1,), (1,)) + jnp.concatenate([o[1], o[2], sh[1], o[3]], axis=1)
    pregate, postscale, postshift, postgate = jnp.split(adapt_own, 4, axis=-1)
    expand_full = jnp.concatenate([rows_of(second_all, i * pr, pr) for i in range(4)], axis=1)
    comb_full = rows_of(second_all, 4 * pr, pr)
    reduce_full = rows_of(second_all, 5 * pr, rr)

    gated = (gating * attended).astype(bf16)
    branch = mm(gated, comb_full, (1,), (0,))
    pregate_sig = jax.nn.sigmoid(pregate)
    residual = tokens + pregate_sig * branch
    post_norm, post_inv = normal_rows(residual)
    post_gain = jax.nn.sigmoid(postscale)
    posthidden = (post_gain * post_norm + postshift).astype(bf16)
    upgate = mm(posthidden, expand_full, (1,), (0,))
    FF = upgate.shape[-1] // 2
    preact, upper = upgate[:, :FF], upgate[:, FF:]
    preact_sig = jax.nn.sigmoid(preact)
    swished = preact * preact_sig
    activated = (swished * upper).astype(bf16)
    trans = mm(activated, reduce_full, (1,), (0,))
    postgate_sig = jax.nn.sigmoid(postgate)
    mixed = (residual + postgate_sig * trans).astype(bf16)

    def owned(grad):
        return [g.reshape(G, T, g.shape[0] // W, D) for g in blocks(grad)]

    g_out = cotangent.reshape(S * R, D)
    trans_back = (postgate_sig * g_out).astype(bf16)
    postgate_back = g_out * trans * slope(postgate_sig)
    reducer_part = mm(activated, trans_back, (0,), (0,), bf16)
    act_back = mm(trans_back, reduce_full, (1,), (1,))
    up_back = jnp.concatenate(
        [act_back * upper * preact_sig * (1.0 + preact * (1.0 - preact_sig)), act_back * swished], axis=-1
    ).astype(bf16)
    expander_part = mm(posthidden, up_back, (0,), (0,), bf16)
    posthidden_back = mm(up_back, expand_full, (1,), (1,))
    postscale_back = posthidden_back * post_norm * slope(post_gain)
    residual_back = g_out + norm_back(post_norm, post_inv, posthidden_back * post_gain)
    branch_back = (pregate_sig * residual_back).astype(bf16)
    pregate_back = residual_back * branch * slope(pregate_sig)
    combiner_part = mm(gated, branch_back, (0,), (0,), bf16)
    second_part = jnp.concatenate(owned(expander_part) + owned(combiner_part) + owned(reducer_part), axis=2)
    second_owned = second_part.reshape(G, -1, D)
    second_part = lax.psum_scatter(second_owned, "samp", scatter_dimension=0, tiled=False)

    gated_back = mm(branch_back, comb_full, (1,), (1,))
    attended_back = (gating * gated_back).astype(bf16)
    gating_low = (attended * gated_back * slope(gating)).astype(bf16)
    query_back, dkv, *bias_back = attention_back(
        me.astype(jnp.int32)[None], probs, attended_back.reshape(S, R, D), kv, query, second_owned, fold, G
    )
    query_back = query_back.reshape(S * R, D)
    dkv = dkv.reshape(S, 2 * D, N)

    later = jnp.concatenate([pregate_back, postscale_back, posthidden_back, postgate_back], axis=-1)
    later_sums = jnp.split(jnp.sum(later, axis=0), 4)
    later_low = later.astype(bf16)
    later_part = mm(later_low, cond_low, (0,), (0,), bf16)
    later_back = mm(later_low, cond_rest, (1,), (0,))

    pre_back_all = mm(dkv, proj_full[:, 2 * D :], (1,), (1,), bf16)
    if fold > 1:
        kept, given = bias_back
        bias_both = (kept.astype(f32) + hop(given, "samp", 1).astype(f32) + zero(pre_back_all).astype(f32)).astype(bf16)
        bias_sum = sum_samp_end(bias_both)
    else:
        bias_sum = sum_samp([bias_back[0].reshape(H * R, G, C).transpose(1, 0, 2)]).reshape(H, R, C)
    qg_low = jnp.concatenate([query_back.astype(bf16), gating_low], axis=-1)
    pair_grad, pairhead_part = pair_back(pairwise[0], bias_sum.transpose(1, 0, 2), pht, fold)
    qg_part = mm(pre, qg_low, (0,), (0,), bf16)
    kv_part = mm(pre_all.reshape(S, N, D), dkv, (0, 1), (0, 2), bf16)
    proj_owned = jnp.concatenate(owned(qg_part) + owned(kv_part), axis=2).reshape(G, -1, D)
    proj_part = lax.psum_scatter(proj_owned, "samp", scatter_dimension=0, tiled=False)
    pre_back = sum_tok(pre_back_all.reshape(S, T, R, D), pairhead_part, proj_owned, dim=1).reshape(S * R, D)
    pre_back = pre_back + mm(qg_low, proj_full[:, : 2 * D], (1,), (1,))

    token_norm, token_inv = normal_rows(tokens)
    gain = own(gain_all)
    prescale_back = pre_back * token_norm * slope(gain)
    tokens_grad = residual_back + norm_back(token_norm, token_inv, pre_back * gain)
    early = jnp.concatenate([prescale_back, pre_back], axis=-1)
    early_sums = jnp.split(jnp.sum(early, axis=0), 2)
    early_low = early.astype(bf16)
    early_part = mm(early_low, cond_low, (0,), (0,), bf16)
    cond_grad = norm_back(cond_norm, cond_inv, later_back + mm(early_low, cond_pre, (1,), (0,)))

    offsets_part = jnp.concatenate([early_sums[0], later_sums[0], later_sums[1], later_sums[3]])
    shifts_part = jnp.concatenate([early_sums[1], later_sums[2]])
    querybias_part = jnp.sum(query_back, axis=0)
    cond_part = jnp.concatenate([early_part, later_part], axis=0).reshape(G, T, cc, CS)
    cond_part = jnp.concatenate([cond_part[:, :, : cc // 2], cond_part[:, :, cc // 2 :]], axis=-1)
    vec_part = jnp.concatenate(
        [offsets_part.reshape(G, T, no), shifts_part.reshape(G, T, ns), querybias_part.reshape(G, T, pr)], axis=-1
    )
    vec_part = jnp.zeros((G, T, 8, D), bf16).at[:, :, 0, : vec.shape[0]].set(vec_part.astype(bf16))
    cond_part = jnp.concatenate([cond_part, vec_part], axis=2).reshape(G, -1, D)
    cond_grad = cond_grad.reshape(S, R, CS)
    singles_part = jnp.sum(cond_grad, axis=0)
    cs = CS // G
    extra = jnp.pad(singles_part.T, ((0, 0), (0, D - R))).reshape(G, cs, D).astype(bf16)
    cond_both = sum_samp_start([cond_part, extra])
    second_part, proj_part = second_part.reshape(T, -1, D), proj_part.reshape(T, -1, D)
    both_part = jnp.concatenate([second_part + zero(cond_part).astype(bf16), proj_part], axis=1)
    both_sum = lax.psum_scatter(both_part, "tok", scatter_dimension=0, tiled=False).astype(f32)
    second_sum, proj_sum = both_sum[: second.shape[0]], both_sum[second.shape[0] :]
    both = sum_samp_end(cond_both)
    cond_sum, singles_t = both[: cond_part.shape[1]], both[cond_part.shape[1] :, :R]
    cond_half = cond_sum
    cond_sum = sum_tok(cond_sum.reshape(T, -1, D))

    by_sample = jnp.concatenate(
        [jnp.sum(cond_grad, axis=1), jnp.broadcast_to(jnp.where(t == 0, noise_level, 0)[:, None], (S, 128)).astype(f32)],
        axis=1,
    )
    placed = lax.dynamic_update_slice_in_dim(jnp.zeros((G * S, CS + 128), f32), by_sample, me * S, 0)
    small = everyone(jnp.concatenate([placed, jnp.pad(pairhead_part, ((0, 0), (0, CS)))], axis=0), cond_half)
    level_all = small[: G * S, CS].astype(jnp.int32)
    levels = jnp.arange(noise_table.shape[0], dtype=jnp.int32)
    level_hot = (levels[:, None] == level_all[None, :]).astype(f32)
    noise_grad = jnp.dot(level_hot, small[: G * S, :CS], precision=lax.Precision.HIGHEST)
    pairhead_grad = small[G * S :, : pairhead_part.shape[1]].T

    def unblocks(x, order):
        return jnp.concatenate([x[i * pr : (i + 1) * pr] for i in order], axis=1)

    cond_out = cond_sum[: cc // 2]
    vec_out = cond_sum[cc // 2]
    return (
        mixed.reshape(S, R, D),
        tokens_grad.reshape(S, R, D),
        singles_t.T[None],
        pair_grad[None],
        noise_grad,
        jnp.concatenate([cond_out[:, :CS], cond_out[:, CS:]], axis=0).T,
        vec_out[:no],
        vec_out[no : no + ns],
        unblocks(proj_sum, (0, 2, 3, 1)),
        vec_out[no + ns : no + ns + pr],
        second_sum[4 * pr : 5 * pr],
        unblocks(second_sum, (0, 1, 2, 3)),
        second_sum[5 * pr :],
        pairhead_grad,
    )


def solution(mesh):
    shard = ("samp", "tok")
    in_specs = (
        P("samp", "tok", None), P("samp", "tok", None), P(None, "tok", None), P(), P("samp"), P(),
        P(None, "tok", "samp", None), P(None, shard), P(shard), P(shard), P(shard, None), P(shard),
        P(shard, None), P(shard, None), P(shard, None), P(),
    )
    out_specs = (
        P("samp", "tok", None), P("samp", "tok", None), P(None, "tok", "samp"), P(None, "tok", "samp", None), P(),
        P(None, shard), P(shard), P(shard), P(shard, None), P(shard), P(shard, None), P(shard, None),
        P(shard, None), P(),
    )
    return jax.shard_map(per_device, mesh=mesh, in_specs=in_specs, out_specs=out_specs, check_vma=False)
```

time: 744 us -> 488 us (0.66)
  local copies, waits for them, and re-layouts: 189 us -> 69.2 us
  waiting for transfers between devices: 215 us -> 131 us
  blocking collectives: 40.2 us -> 0 us
  starting transfers between devices: 31.7 us -> 62.3 us
  matrix products: 87.1 us -> 65.9 us
  other arithmetic: 57.1 us -> 39.6 us
    all_gather x1, waiting for transfers between devices: 71.9 us -> 0.02 us  [per_device(): first_all = lax.all_gather(first, ('samp', 'tok'), axis=0)]
    unnamed x191 -> x160, local copies, waits for them, and re-layouts: 61.6 us -> 21.4 us
    psum x1 -> x0, blocking collectives: 40.2 us -> none  [per_device(): lax.psum((noise_part, pairhead_part), ('samp', 'tok'))]
    all_gather x2 -> x1, waiting for transfers between devices: 34.2 us -> 0.01 us  [per_device(): lax.all_gather(second_mine, 'samp', axis=0).reshape(W, second.shape[0], D)]
    ppermute x28 -> x32, starting transfers between devices: 31.5 us -> 61.6 us  [the longest x26 36.3 us: hop(): lax.ppermute(x, axis, [(i, i ^ k) for i in range(lax.axis_size(axis))])]
    reshape x4 -> x1, local copies, waits for them, and re-layouts: 25.7 us -> 0.06 us  [per_device(): first_all[:, -single_rows:].reshape(G, T, single_rows, D)]
    dot_general x25 -> x22, matrix products: 85.9 us -> 64.9 us  [mm(): lax.dot_general(a, b, ((ca, cb), ((), ())), preferred_element_type=f32)]
    ppermute x28 -> x32, waiting for transfers between devices: 109 us -> 125 us  [the longest x26 72.7 us: hop(): lax.ppermute(x, axis, [(i, i ^ k) for i in range(lax.axis_size(axis))])]
  transfers between devices with their start and end apart: 32 -> 37, of which waited for: 12 -> 20; matrix products, arithmetic and copies ran while one was open for 30% -> 25% of each run, Pallas kernels for 5% -> 18%
where the time goes in v2:
time: 488 us; the launch traced here: 482 us
  waiting for transfers between devices  131 us (27%)
  Pallas kernels  89 us (18%)
  local copies, waits for them, and re-layouts  69.2 us (14%)
  matrix products  65.9 us (14%)
  starting transfers between devices  62.3 us (13%)
  other arithmetic  39.6 us (8%)
  between operations  24 us (5%)
    ppermute x26, waiting for transfers between devices, hop(): lax.ppermute(x, axis, [(i, i ^ k) for i in range(lax.axis_size(axis))])  72.7 us
    dot_general x22, matrix products, mm(): lax.dot_general(a, b, ((ca, cb), ((), ())), preferred_element_type=f32)  64.9 us
    ppermute x26, starting transfers between devices, hop(): lax.ppermute(x, axis, [(i, i ^ k) for i in range(lax.axis_size(axis))])  36.3 us
    ppermute x3, waiting for transfers between devices, gather_tok(): lax.ppermute(down[-1], 'tok', [(i + 1, i) for i in range(n - 1)])  27.5 us
    ppermute x3, waiting for transfers between devices, gather_tok(): up.append(lax.ppermute(up[-1], 'tok', [(i, i + 1) for i in range(n - 1)]))  25.3 us
    pallas_call x1, Pallas kernels, attention_back(): pl.pallas_call(body, grid_spec=pltpu.PrefetchScalarGridSpec(num_scalar_pr...  25 us
    pallas_call x1, Pallas kernels, attention(): pl.pallas_call(attention_body, grid=(H,), in_specs=[whole(S, R, D), whole...  24.4 us
    ppermute x3, starting transfers between devices, gather_tok(): up.append(lax.ppermute(up[-1], 'tok', [(i, i + 1) for i in range(n - 1)]))  21.5 us
  transfers between devices with their start and end apart: 37, of which 20 were waited for; matrix products, arithmetic and copies ran while one was open for 25% of the time, Pallas kernels for 18%

profile of v2, /device:TPU:0, one launch (start us, length us, event | category | flops | bytes accessed | tf_op | source)
XLA Modules:
  0.0 481.6 jit_solution(11919482762723864602)
XLA Ops:
  16.2 8.9 %pair_bias.1.refs_0_ = bf16[16,48,384]{2,1,0:T(8,128)(2,1)} custom-call(bf16[4,48,96,128]{3,2,1,0:T(8,128)(2,1)} %bitcast.280, bf16[16,128]{1,0:T(8,128)(2,1)} %bitcast.353), custom_call_target="tpu_custom_call" | custom-call | flops 1024 | bytes 1024 | tf_op jit(solution)/shard_map/pair_bias/pallas_call | solution.py:192
  25.1 3.9 collective-permute-start.5
  29.0 4.6 collective-permute-start.7
  33.6 11.4 %collective-permute-done.8 = bf16[552,768]{1,0:T(8,128)(2,1)S(1)} collective-permute-done((bf16[552,768]{1,0:T(8,128)(2,1)S(1)}, bf16[552,768]{1,0:T(8,128)(2,1)S(1)}, u32[]{:S(2)}, u32[]{:S(2)}) %collective-permute-start.8) | collective-permute-done | bytes 847904 | tf_op jit(solution)/shard_map/ppermute | solution.py:375
  46.3 1.7 collective-permute-start.3
  49.5 11.2 %collective-permute-done.7 = bf16[552,768]{1,0:T(8,128)(2,1)S(1)} collective-permute-done((bf16[552,768]{1,0:T(8,128)(2,1)S(1)}, bf16[552,768]{1,0:T(8,128)(2,1)S(1)}, u32[]{:S(2)}, u32[]{:S(2)}) %collective-permute-start.7) | collective-permute-done | bytes 847904 | tf_op jit(solution)/shard_map/ppermute | solution.py:374
  60.7 5.5 %collective-permute-start.11 = (bf16[552,768]{1,0:T(8,128)(2,1)S(1)}, bf16[552,768]{1,0:T(8,128)(2,1)}, u32[]{:S(2)}, u32[]{:S(2)}) collective-permute-start(bf16[552,768]{1,0:T(8,128)(2,1)S(1)} %collective-permute-done.7), channel_id=1, source_target_pairs={{0,1},{1,2},{2,3},{4,5},{5,6},{6,7},{8,9},{9,10},{10,11},{12,13},{... | collective-permute-start | bytes 2543624 | tf_op jit(solution)/shard_map/ppermute | solution.py:374
  66.2 3.7 collective-permute-done.1.refs_2_
  70.4 9.3 %collective-permute-done.9 = bf16[552,768]{1,0:T(8,128)(2,1)} collective-permute-done((bf16[552,768]{1,0:T(8,128)(2,1)S(1)}, bf16[552,768]{1,0:T(8,128)(2,1)}, u32[]{:S(2)}, u32[]{:S(2)}) %collective-permute-start.9) | collective-permute-done | bytes 847904 | tf_op jit(solution)/shard_map/ppermute | solution.py:375
  81.0 12.9 %collective-permute-done.11 = bf16[552,768]{1,0:T(8,128)(2,1)} collective-permute-done((bf16[552,768]{1,0:T(8,128)(2,1)S(1)}, bf16[552,768]{1,0:T(8,128)(2,1)}, u32[]{:S(2)}, u32[]{:S(2)}) %collective-permute-start.11) | collective-permute-done | bytes 847904 | tf_op jit(solution)/shard_map/ppermute | solution.py:374
  93.9 11.4 %collective-permute-start.12 = (bf16[552,768]{1,0:T(8,128)(2,1)}, bf16[552,768]{1,0:T(8,128)(2,1)}, u32[]{:S(2)}, u32[]{:S(2)}) collective-permute-start(bf16[552,768]{1,0:T(8,128)(2,1)} %collective-permute-done.11), channel_id=1, source_target_pairs={{0,1},{1,2},{2,3},{4,5},{5,6},{6,7},{8,9},{9,10},{10,11},{12,13},{... | collective-permute-start | bytes 2543624 | tf_op jit(solution)/shard_map/ppermute | solution.py:374
  105.3 9.9 %lay_bias.1.bias_ref = bf16[16,192,768]{2,1,0:T(8,128)(2,1)} custom-call(s32[1]{0:T(128)} %bitcast.18.me_ref, bf16[16,48,384]{2,1,0:T(8,128)(2,1)} %pair_bias.1.refs_0_, bf16[16,48,384]{2,1,0:T(8,128)(2,1)} %copy-done.46, bf16[16,48,384]{2,1,0:T(8,128)(2,1)} %copy-done.45, bf16[16,48,384]{2,1,0:T(8,128)(2,1)} %collective-permute-done.2.refs_3_, ...), custom_call_target="tpu_custom_call" | custom-call | flops 1024 | bytes 1024 | tf_op jit(solution)/shard_map/lay_bias/pallas_call | solution.py:291
  118.6 6.8 %collective-permute-done.10 = bf16[552,768]{1,0:T(8,128)(2,1)} collective-permute-done((bf16[552,768]{1,0:T(8,128)(2,1)}, bf16[552,768]{1,0:T(8,128)(2,1)}, u32[]{:S(2)}, u32[]{:S(2)}) %collective-permute-start.10) | collective-permute-done | bytes 847904 | tf_op jit(solution)/shard_map/ppermute | solution.py:375
  142.9 2.1 slice.503
  149.8 2.5 copy.95
  152.2 1.8 lay_vectors.1
  159.7 2.7 convolution_add_fusion
  162.4 3.8 fusion.4
  169.5 5.8 %convolution_convert_fusion = bf16[1536,1536]{1,0:T(8,128)(2,1)} fusion(bf16[1536,768]{1,0:T(8,128)(2,1)S(1)} %get-tuple-element.68, bf16[768,768]{1,0:T(8,128)(2,1)S(1)} %bitcast.331, bf16[768,768]{1,0:T(8,128)(2,1)S(1)} %bitcast.329), kind=kOutput, calls=%fused_computation.3 | convolution fusion | flops 3630956544 | bytes 9437184 | tf_op jit(solution)/shard_map/dot_general | solution.py:345
  175.3 24.4 %attention.1 = (bf16[16,2,192,768]{3,2,1,0:T(8,128)(2,1)}, f32[2,192,768]{2,1,0:T(8,128)}) custom-call(bf16[2,192,768]{2,1,0:T(8,128)(2,1)} %bitcast.320, bf16[2,768,1536]{2,1,0:T(8,128)(2,1)} %bitcast.273, bf16[2,768,1536]{2,1,0:T(8,128)(2,1)} %bitcast.274, bf16[16,192,768]{2,1,0:T(8,128)(2,1)} %lay_bias.1.bias_ref, f32[1,768]{1,0:T(1,128)} %add_multiply_fusion.mask_ref), custom_call_target="tpu_custom_call" | custom-call | flops 1024 | bytes 1024 | tf_op jit(solution)/shard_map/attention/pallas_call | solution.py:51
  199.7 1.9 fusion.108
  202.9 1.9 fusion.65
  204.9 3.6 convolution_add_fusion.1
  208.5 3.2 fusion.111
  216.1 2.0 fusion.70
  218.1 1.8 slice.518
  220.0 1.9 multiply_convert_fusion.1
  221.8 3.8 fusion.103
  225.6 3.0 convolution_convert_fusion.1
  230.0 3.5 fusion.46
  243.8 2.5 constant_dynamic-slice_fusion
  246.4 3.3 fusion.45
  249.7 25.0 %attention_back.1 = (f32[2,192,768]{2,1,0:T(8,128)}, bf16[2,2,768,768]{3,2,1,0:T(8,128)(2,1)}, bf16[4,16,48,384]{3,2,1,0:T(8,128)(2,1)}, bf16[4,16,48,384]{3,2,1,0:T(8,128)(2,1)}) custom-call(s32[1]{0:T(128)} %bitcast.18.me_ref, bf16[16,2,192,768]{3,2,1,0:T(8,128)(2,1)} %get-tuple-element.47.p_ref, bf16[2,192,768]{2,1,0:T(8,128)(2,1)} %bitcast.322, ...), custom_call_target="tpu_custom_call" | custom-call | flops 1024 | bytes 1024 | tf_op jit(solution)/shard_map/attention_back/pallas_call | solution.py:132
  274.7 3.7 copy.101
  280.8 8.0 %fusion.23 = bf16[2,768,768]{2,1,0:T(8,128)(2,1)} fusion(bf16[2,1536,768]{2,1,0:T(8,128)(2,1)} %bitcast.356, bf16[768,768]{1,0:T(8,128)(2,1)S(1)} %bitcast.332, bf16[768,768]{1,0:T(8,128)(2,1)S(1)} %bitcast.330), kind=kOutput, calls=%fused_computation.56 | convolution fusion | flops 3629776896 | bytes 9437184 | tf_op jit(solution)/shard_map/dot_general | solution.py:345
  290.8 3.0 convolution_convert_fusion.3
  293.8 6.6 %bitcast_convert_fusion = bf16[768,1536]{1,0:T(8,128)(2,1)S(1)} fusion(bf16[2,768,768]{2,1,0:T(8,128)(2,1)S(1)} %bitcast.308, bf16[2,1536,768]{2,1,0:T(8,128)(2,1)} %bitcast.357), kind=kOutput, calls=%fused_computation.14 | convolution fusion | flops 3625058304 | bytes 9437184 | tf_op jit(solution)/shard_map/dot_general | solution.py:345
  300.8 2.7 pad_maximum_fusion.1
  305.3 3.2 add_convert_fusion
  310.5 2.3 fusion.20
  315.5 2.8 collective-permute-start.17
  318.3 5.7 %collective-permute-start.19 = (bf16[2,192,768]{2,1,0:T(8,128)(2,1)S(1)}, bf16[2,192,768]{2,1,0:T(8,128)(2,1)}, u32[]{:S(2)}, u32[]{:S(2)}) collective-permute-start(bf16[2,192,768]{2,1,0:T(8,128)(2,1)S(1)} %get-tuple-element.110), channel_id=1, source_target_pairs={{0,3},{1,2},{2,1},{3,0},{4,7},{5,6},{6,5},{7,4},{8,11},{9,10},{10,... | collective-permute-start | bytes 1769480 | tf_op jit(solution)/shard_map/ppermute | solution.py:349
  324.0 5.6 %collective-permute-done.14 = bf16[16,48,384]{2,0,1:T(8,128)(2,1)S(1)} collective-permute-done((bf16[16,48,384]{2,0,1:T(8,128)(2,1)S(1)}, bf16[16,48,384]{2,0,1:T(8,128)(2,1)S(1)}, u32[]{:S(2)}, u32[]{:S(2)}) %collective-permute-start.14) | collective-permute-done | bytes 589856 | tf_op jit(solution)/shard_map/ppermute | solution.py:349
  329.6 2.3 collective-permute-start.18
  331.9 3.1 convolution_convert_fusion.2
  335.0 7.9 %collective-permute-done.16 = bf16[16,48,384]{2,0,1:T(8,128)(2,1)S(1)} collective-permute-done((bf16[16,48,384]{2,0,1:T(8,128)(2,1)S(1)}, bf16[16,48,384]{2,0,1:T(8,128)(2,1)S(1)}, u32[]{:S(2)}, u32[]{:S(2)}) %collective-permute-start.16) | collective-permute-done | bytes 589856 | tf_op jit(solution)/shard_map/ppermute | solution.py:349
  344.3 19.1 %pair_back.1 = (f32[4,48,96,128]{3,2,1,0:T(8,128)}, f32[16,128]{1,0:T(8,128)}) custom-call(bf16[4,48,96,128]{3,2,1,0:T(8,128)(2,1)} %bitcast.281, f32[48,16,384]{2,1,0:T(8,128)} %fusion.63.bb_ref, bf16[16,128]{1,0:T(8,128)(2,1)} %bitcast.354), custom_call_target="tpu_custom_call" | custom-call | flops 1024 | bytes 1024 | tf_op jit(solution)/shard_map/pair_back/pallas_call | solution.py:246
  365.4 10.4 %collective-permute-done.18 = bf16[2,192,768]{2,1,0:T(8,128)(2,1)} collective-permute-done((bf16[2,192,768]{2,1,0:T(8,128)(2,1)S(1)}, bf16[2,192,768]{2,1,0:T(8,128)(2,1)}, u32[]{:S(2)}, u32[]{:S(2)}) %collective-permute-start.18) | collective-permute-done | bytes 589856 | tf_op jit(solution)/shard_map/ppermute | solution.py:349
  375.7 1.9 fusion.60
  377.6 2.7 fusion.99
  383.0 2.3 fusion.105
  390.5 3.2 collective-permute-done.20
  400.3 5.9 %reduce-scatter.6.cloned.1.call-done = bf16[1,384,768]{2,1,0:T(8,128)(2,1)} async-done(((bf16[8,384,768]{2,1,0:T(8,128)(2,1)}), bf16[1,384,768]{2,1,0:T(8,128)(2,1)}) %reduce-scatter.6.cloned.1.call-update) | async-done | bytes 589840 | tf_op jit(solution)/shard_map/reduce_scatter | solution.py:608
  406.2 2.4 pad_maximum_fusion.9
  408.7 3.3 collective-permute-start.24
  412.0 2.2 collective-permute-done.21
  414.2 12.7 %collective-permute-done.23 = bf16[368,768]{1,0:T(8,128)(2,1)} collective-permute-done((bf16[368,768]{1,0:T(8,128)(2,1)}, bf16[368,768]{1,0:T(8,128)(2,1)}, u32[]{:S(2)}, u32[]{:S(2)}) %collective-permute-start.23) | collective-permute-done | bytes 565280 | tf_op jit(solution)/shard_map/ppermute | solution.py:349
  429.9 2.4 collective-permute-start.25
  436.6 3.6 collective-permute-done.25
  440.3 6.3 %collective-permute-done.29 = bf16[80,768]{1,0:T(8,128)(2,1)S(1)} collective-permute-done((bf16[80,768]{1,0:T(8,128)(2,1)S(1)}, bf16[80,768]{1,0:T(8,128)(2,1)S(1)}, u32[]{:S(2)}, u32[]{:S(2)}) %collective-permute-start.29) | collective-permute-done | bytes 122912 | tf_op jit(solution)/shard_map/ppermute | solution.py:349
  446.7 2.1 collective-permute-done.31
  448.7 10.6 %collective-permute-done.30 = bf16[80,768]{1,0:T(8,128)(2,1)S(1)} collective-permute-done((bf16[80,768]{1,0:T(8,128)(2,1)S(1)}, bf16[80,768]{1,0:T(8,128)(2,1)S(1)}, u32[]{:S(2)}, u32[]{:S(2)}) %collective-permute-start.30) | collective-permute-done | bytes 122912 | tf_op jit(solution)/shard_map/ppermute | solution.py:349
  462.7 2.2 collective-permute-done.27
  467.1 2.1 collective-permute-done.28
  (358 shorter events, 103.6 us)
Async XLA Ops:
  7.2 7.6 %copy-start.50 = (bf16[24,3072]{1,0:T(8,128)(2,1)S(1)}, bf16[24,3072]{1,0:T(8,128)(2,1)}, u32[]{:S(2)}) copy-start(bf16[24,3072]{1,0:T(8,128)(2,1)} %param.33) | copy-start | bytes 442372
  7.2 7.7 %copy-start.52 = (bf16[24,768]{1,0:T(8,128)(2,1)S(1)}, bf16[24,768]{1,0:T(8,128)(2,1)}, u32[]{:S(2)}) copy-start(bf16[24,768]{1,0:T(8,128)(2,1)} %param.32) | copy-start | bytes 110596
  7.2 7.7 %copy-start.51 = (bf16[48,768]{1,0:T(8,128)(2,1)S(1)}, bf16[48,768]{1,0:T(8,128)(2,1)}, u32[]{:S(2)}) copy-start(bf16[48,768]{1,0:T(8,128)(2,1)} %param.34) | copy-start | bytes 221188
  7.2 122.6 %all-gather.8.cloned.1.call-start = ((), (), s32[]{:S(2)}) async-start(), calls=%async_computation.7 | async-start | bytes 9732096 | tf_op jit(solution)/shard_map/all_gather | solution.py:475
  13.6 194.9 %all-gather.6.cloned.1.call-start = ((), (), s32[]{:S(2)}) async-start(), calls=%async_computation.6 | async-start | bytes 9289728 | tf_op jit(solution)/shard_map/all_gather | solution.py:488
  14.9 14.1 %copy-start.13 = (bf16[552,768]{1,0:T(8,128)(2,1)}, bf16[552,768]{1,0:T(8,128)(2,1)S(1)}, u32[]{:S(2)}) copy-start(bf16[552,768]{1,0:T(8,128)(2,1)S(1)} %constant_dynamic-update-slice_fusion.6) | copy-start | bytes 2543620
  14.9 30.1 %collective-permute-start.8 = (bf16[552,768]{1,0:T(8,128)(2,1)S(1)}, bf16[552,768]{1,0:T(8,128)(2,1)S(1)}, u32[]{:S(2)}, u32[]{:S(2)}) collective-permute-start(bf16[552,768]{1,0:T(8,128)(2,1)S(1)} %constant_dynamic-update-slice_fusion.6), channel_id=1, source_target_pairs={{1,0},{2,1},{3,2},{5,4},{6,5},{7,6},{9,8},{10,9},{11,10},{13,12},{... | collective-permute-start | bytes 2543624 | tf_op jit(solution)/shard_map/ppermute | solution.py:375
  25.1 24.4 %collective-permute-start.5 = (bf16[16,48,384]{2,1,0:T(8,128)(2,1)}, bf16[16,48,384]{2,1,0:T(8,128)(2,1)S(1)}, u32[]{:S(2)}, u32[]{:S(2)}) collective-permute-start(bf16[16,48,384]{2,1,0:T(8,128)(2,1)} %pair_bias.1.refs_0_), channel_id=1, source_target_pairs={{0,24},{4,28},{8,16},{12,20},{16,8},{20,12},{24,0},{28,4},{1,25},{... | collective-permute-start | bytes 1769480 | tf_op jit(solution)/shard_map/ppermute | solution.py:349
  29.0 31.7 %collective-permute-start.7 = (bf16[552,768]{1,0:T(8,128)(2,1)S(1)}, bf16[552,768]{1,0:T(8,128)(2,1)S(1)}, u32[]{:S(2)}, u32[]{:S(2)}) collective-permute-start(bf16[552,768]{1,0:T(8,128)(2,1)S(1)} %constant_dynamic-update-slice_fusion.6), channel_id=1, source_target_pairs={{0,1},{1,2},{2,3},{4,5},{5,6},{6,7},{8,9},{9,10},{10,11},{12,13},{... | collective-permute-start | bytes 2543624 | tf_op jit(solution)/shard_map/ppermute | solution.py:374
  45.0 15.7 %copy-start.39 = (bf16[552,768]{1,0:T(8,128)(2,1)}, bf16[552,768]{1,0:T(8,128)(2,1)S(1)}, u32[]{:S(2)}) copy-start(bf16[552,768]{1,0:T(8,128)(2,1)S(1)} %collective-permute-done.8) | copy-start | bytes 2543620
  45.0 34.7 %collective-permute-start.9 = (bf16[552,768]{1,0:T(8,128)(2,1)S(1)}, bf16[552,768]{1,0:T(8,128)(2,1)}, u32[]{:S(2)}, u32[]{:S(2)}) collective-permute-start(bf16[552,768]{1,0:T(8,128)(2,1)S(1)} %collective-permute-done.8), channel_id=1, source_target_pairs={{1,0},{2,1},{3,2},{5,4},{6,5},{7,6},{9,8},{10,9},{11,10},{13,12},{... | collective-permute-start | bytes 2543624 | tf_op jit(solution)/shard_map/ppermute | solution.py:375
  46.3 19.9 %collective-permute-start.3 = (bf16[16,48,384]{2,1,0:T(8,128)(2,1)}, bf16[16,48,384]{2,1,0:T(8,128)(2,1)S(1)}, u32[]{:S(2)}, u32[]{:S(2)}) collective-permute-start(bf16[16,48,384]{2,1,0:T(8,128)(2,1)} %pair_bias.1.refs_0_), channel_id=1, source_target_pairs={{0,16},{4,20},{8,24},{12,28},{16,0},{20,4},{24,8},{28,12},{1,17},{... | collective-permute-start | bytes 1769480 | tf_op jit(solution)/shard_map/ppermute | solution.py:349
  48.0 21.8 %collective-permute-start.1 = (bf16[16,48,384]{2,1,0:T(8,128)(2,1)}, bf16[16,48,384]{2,1,0:T(8,128)(2,1)S(1)}, u32[]{:S(2)}, u32[]{:S(2)}) collective-permute-start(bf16[16,48,384]{2,1,0:T(8,128)(2,1)} %pair_bias.1.refs_0_), channel_id=1, source_target_pairs={{0,8},{4,12},{8,0},{12,4},{16,24},{20,28},{24,16},{28,20},{1,9},{5... | collective-permute-start | bytes 1769480 | tf_op jit(solution)/shard_map/ppermute | solution.py:349
  49.5 55.8 %copy-start.43 = (bf16[16,48,384]{2,1,0:T(8,128)(2,1)}, bf16[16,48,384]{2,1,0:T(8,128)(2,1)S(1)}, u32[]{:S(2)}) copy-start(bf16[16,48,384]{2,1,0:T(8,128)(2,1)S(1)} %collective-permute-done.5.refs_6_) | copy-start | bytes 1769476
  49.5 20.3 %collective-permute-start = (bf16[16,48,384]{2,1,0:T(8,128)(2,1)}, bf16[16,48,384]{2,1,0:T(8,128)(2,1)S(1)}, u32[]{:S(2)}, u32[]{:S(2)}) collective-permute-start(bf16[16,48,384]{2,1,0:T(8,128)(2,1)} %pair_bias.1.refs_0_), channel_id=1, source_target_pairs={{0,4},{4,0},{8,12},{12,8},{16,20},{20,16},{24,28},{28,24},{1,5},{5... | collective-permute-start | bytes 1769480 | tf_op jit(solution)/shard_map/ppermute | solution.py:349
  60.7 54.5 %copy-start.41 = (bf16[552,768]{1,0:T(8,128)(2,1)}, bf16[552,768]{1,0:T(8,128)(2,1)S(1)}, u32[]{:S(2)}) copy-start(bf16[552,768]{1,0:T(8,128)(2,1)S(1)} %collective-permute-done.7) | copy-start | bytes 2543620
  60.7 33.2 %collective-permute-start.11 = (bf16[552,768]{1,0:T(8,128)(2,1)S(1)}, bf16[552,768]{1,0:T(8,128)(2,1)}, u32[]{:S(2)}, u32[]{:S(2)}) collective-permute-start(bf16[552,768]{1,0:T(8,128)(2,1)S(1)} %collective-permute-done.7), channel_id=1, source_target_pairs={{0,1},{1,2},{2,3},{4,5},{5,6},{6,7},{8,9},{9,10},{10,11},{12,13},{... | collective-permute-start | bytes 2543624 | tf_op jit(solution)/shard_map/ppermute | solution.py:374
  66.2 39.1 %copy-start.44 = (bf16[16,48,384]{2,1,0:T(8,128)(2,1)}, bf16[16,48,384]{2,1,0:T(8,128)(2,1)S(1)}, u32[]{:S(2)}) copy-start(bf16[16,48,384]{2,1,0:T(8,128)(2,1)S(1)} %collective-permute-done.3.refs_4_) | copy-start | bytes 1769476
  66.2 39.1 %collective-permute-start.6 = (bf16[16,48,384]{2,1,0:T(8,128)(2,1)S(1)}, bf16[16,48,384]{2,1,0:T(8,128)(2,1)}, u32[]{:S(2)}, u32[]{:S(2)}) collective-permute-start(bf16[16,48,384]{2,1,0:T(8,128)(2,1)S(1)} %collective-permute-done.5.refs_6_), channel_id=1, source_target_pairs={{0,4},{4,0},{8,12},{12,8},{16,20},{20,16},{24,28},{28,24},{1,5},{5... | collective-permute-start | bytes 1769480 | tf_op jit(solution)/shard_map/ppermute | solution.py:349
  69.9 35.4 %copy-start.45 = (bf16[16,48,384]{2,1,0:T(8,128)(2,1)}, bf16[16,48,384]{2,1,0:T(8,128)(2,1)S(1)}, u32[]{:S(2)}) copy-start(bf16[16,48,384]{2,1,0:T(8,128)(2,1)S(1)} %collective-permute-done.1.refs_2_) | copy-start | bytes 1769476
  69.9 35.4 %collective-permute-start.4 = (bf16[16,48,384]{2,1,0:T(8,128)(2,1)S(1)}, bf16[16,48,384]{2,1,0:T(8,128)(2,1)}, u32[]{:S(2)}, u32[]{:S(2)}) collective-permute-start(bf16[16,48,384]{2,1,0:T(8,128)(2,1)S(1)} %collective-permute-done.3.refs_4_), channel_id=1, source_target_pairs={{0,4},{4,0},{8,12},{12,8},{16,20},{20,16},{24,28},{28,24},{1,5},{5... | collective-permute-start | bytes 1769480 | tf_op jit(solution)/shard_map/ppermute | solution.py:349
  69.9 35.4 %copy-start.46 = (bf16[16,48,384]{2,1,0:T(8,128)(2,1)}, bf16[16,48,384]{2,1,0:T(8,128)(2,1)S(1)}, u32[]{:S(2)}) copy-start(bf16[16,48,384]{2,1,0:T(8,128)(2,1)S(1)} %collective-permute-done.refs_1_) | copy-start | bytes 1769476
  69.9 35.4 %collective-permute-start.2 = (bf16[16,48,384]{2,1,0:T(8,128)(2,1)S(1)}, bf16[16,48,384]{2,1,0:T(8,128)(2,1)}, u32[]{:S(2)}, u32[]{:S(2)}) collective-permute-start(bf16[16,48,384]{2,1,0:T(8,128)(2,1)S(1)} %collective-permute-done.1.refs_2_), channel_id=1, source_target_pairs={{0,4},{4,0},{8,12},{12,8},{16,20},{20,16},{24,28},{28,24},{1,5},{5... | collective-permute-start | bytes 1769480 | tf_op jit(solution)/shard_map/ppermute | solution.py:349
  79.7 45.7 %collective-permute-start.10 = (bf16[552,768]{1,0:T(8,128)(2,1)}, bf16[552,768]{1,0:T(8,128)(2,1)}, u32[]{:S(2)}, u32[]{:S(2)}) collective-permute-start(bf16[552,768]{1,0:T(8,128)(2,1)} %collective-permute-done.9), channel_id=1, source_target_pairs={{1,0},{2,1},{3,2},{5,4},{6,5},{7,6},{9,8},{10,9},{11,10},{13,12},{... | collective-permute-start | bytes 2543624 | tf_op jit(solution)/shard_map/ppermute | solution.py:375
  93.9 35.6 %collective-permute-start.12 = (bf16[552,768]{1,0:T(8,128)(2,1)}, bf16[552,768]{1,0:T(8,128)(2,1)}, u32[]{:S(2)}, u32[]{:S(2)}) collective-permute-start(bf16[552,768]{1,0:T(8,128)(2,1)} %collective-permute-done.11), channel_id=1, source_target_pairs={{0,1},{1,2},{2,3},{4,5},{5,6},{6,7},{8,9},{9,10},{10,11},{12,13},{... | collective-permute-start | bytes 2543624 | tf_op jit(solution)/shard_map/ppermute | solution.py:374
  117.1 8.3 %copy-start.42 = (bf16[552,768]{1,0:T(8,128)(2,1)S(1)}, bf16[552,768]{1,0:T(8,128)(2,1)}, u32[]{:S(2)}) copy-start(bf16[552,768]{1,0:T(8,128)(2,1)} %copy-done.41) | copy-start | bytes 2543620
  129.8 9.3 %copy-start.1 = (bf16[4,552,768]{2,1,0:T(8,128)(2,1)}, bf16[4,552,768]{2,1,0:T(8,128)(2,1)S(1)}, u32[]{:S(2)}) copy-start(bf16[4,552,768]{2,1,0:T(8,128)(2,1)S(1)} %bitcast_dynamic-update-slice_fusion) | copy-start | bytes 10174468
  129.8 9.3 %copy-start.49 = (bf16[1,192,384]{2,1,0:T(8,128)(2,1)S(1)}, bf16[1,192,384]{2,1,0:T(8,128)(2,1)}, u32[]{:S(2)}) copy-start(bf16[1,192,384]{2,1,0:T(8,128)(2,1)} %param.22) | copy-start | bytes 442372
  133.3 7.9 %copy-start.62 = (s32[1,768]{1,0:T(1,128)S(1)}, s32[1,768]{1,0:T(1,128)}, u32[]{:S(2)}) copy-start(s32[1,768]{1,0:T(1,128)} %param.25) | copy-start | bytes 9220
  133.3 265.7 %reduce-scatter.4.cloned.1.call-start = ((), (), s32[]{:S(2)}) async-start(), calls=%async_computation.3 | async-start | bytes 9289728 | tf_op jit(solution)/shard_map/reduce_scatter | solution.py:579
  159.6 6.6 %slice-start.2 = ((s8[9437184]{0:T(1024)(128)(4,1)}), s8[4194304]{0:T(1024)(128)(4,1)S(1)}, s32[]{:S(2)}) async-start(s8[9437184]{0:T(1024)(128)(4,1)} %bitcast.292), calls=%async_computation.10 | async-start | bytes 8388608
  159.6 6.6 %slice-start.3 = ((s8[9437184]{0:T(1024)(128)(4,1)}), s8[4194304]{0:T(1024)(128)(4,1)S(1)}, s32[]{:S(2)}) async-start(s8[9437184]{0:T(1024)(128)(4,1)} %bitcast.292), calls=%async_computation.11 | async-start | bytes 8388608
  166.3 35.6 %copy-start.47 = (bf16[2,192,768]{2,1,0:T(8,128)(2,1)}, bf16[2,192,768]{2,1,0:T(8,128)(2,1)S(1)}, u32[]{:S(2)}) copy-start(bf16[2,192,768]{2,1,0:T(8,128)(2,1)S(1)} %constant_dynamic-slice_fusion.2) | copy-start | bytes 1769476
  166.6 8.7 %copy-start.24 = (bf16[32,24,768]{2,1,0:T(8,128)(2,1)}, bf16[32,24,768]{2,1,0:T(8,128)(2,1)S(1)}, u32[]{:S(2)}) copy-start(bf16[32,24,768]{2,1,0:T(8,128)(2,1)S(1)} %get-tuple-element.71) | copy-start | bytes 3538948
  166.6 8.6 %copy-start.26 = (bf16[32,24,768]{2,1,0:T(8,128)(2,1)}, bf16[32,24,768]{2,1,0:T(8,128)(2,1)S(1)}, u32[]{:S(2)}) copy-start(bf16[32,24,768]{2,1,0:T(8,128)(2,1)S(1)} %get-tuple-element.72) | copy-start | bytes 3538948
  166.7 35.3 %copy-start.22 = (bf16[32,24,768]{2,1,0:T(8,128)(2,1)}, bf16[32,24,768]{2,1,0:T(8,128)(2,1)S(1)}, u32[]{:S(2)}) copy-start(bf16[32,24,768]{2,1,0:T(8,128)(2,1)S(1)} %get-tuple-element.74) | copy-start | bytes 3538948
  208.5 4.5 copy-start
  208.5 4.8 %copy-start.65 = (bf16[384,768]{1,0:T(8,128)(2,1)S(1)}, bf16[384,768]{1,0:T(8,128)(2,1)}, u32[]{:S(2)}) copy-start(bf16[384,768]{1,0:T(8,128)(2,1)} %get-tuple-element.158) | copy-start | bytes 1769476
  243.1 163.1 %reduce-scatter.6.cloned.1.call-start = ((), (), s32[]{:S(2)}) async-start(), calls=%async_computation.4 | async-start | bytes 5308416 | tf_op jit(solution)/shard_map/reduce_scatter | solution.py:608
  278.4 26.9 %collective-permute-start.13 = (bf16[4,16,48,384]{3,1,2,0:T(8,128)(2,1)}, bf16[4,16,48,384]{3,1,2,0:T(8,128)(2,1)}, u32[]{:S(2)}, u32[]{:S(2)}) collective-permute-start(bf16[4,16,48,384]{3,1,2,0:T(8,128)(2,1)} %copy.101), channel_id=1, source_target_pairs={{0,4},{4,0},{8,12},{12,8},{16,20},{20,16},{24,28},{28,24},{1,5},{5... | collective-permute-start | bytes 7077896 | tf_op jit(solution)/shard_map/ppermute | solution.py:349
  278.8 10.0 %copy-start.53 = (bf16[3072]{0:T(1024)(128)(2,1)}, bf16[3072]{0:T(1024)(128)(2,1)S(1)}, u32[]{:S(2)}) copy-start(bf16[3072]{0:T(1024)(128)(2,1)S(1)} %fusion.8) | copy-start | bytes 18436
  308.7 5.9 %copy-start.15 = (bf16[2,768,768]{2,1,0:T(8,128)(2,1)S(1)}, bf16[2,768,768]{2,1,0:T(8,128)(2,1)}, u32[]{:S(2)}) copy-start(bf16[2,768,768]{2,1,0:T(8,128)(2,1)} %fusion.23) | copy-start | bytes 7077892
  308.7 20.9 %collective-permute-start.14 = (bf16[16,48,384]{2,0,1:T(8,128)(2,1)S(1)}, bf16[16,48,384]{2,0,1:T(8,128)(2,1)S(1)}, u32[]{:S(2)}, u32[]{:S(2)}) collective-permute-start(bf16[16,48,384]{2,0,1:T(8,128)(2,1)S(1)} %get-tuple-element.106), channel_id=1, source_target_pairs={{0,8},{4,12},{8,0},{12,4},{16,24},{20,28},{24,16},{28,20},{1,9},{5... | collective-permute-start | bytes 1769480 | tf_op jit(solution)/shard_map/ppermute | solution.py:349
  312.8 30.1 %collective-permute-start.16 = (bf16[16,48,384]{2,0,1:T(8,128)(2,1)S(1)}, bf16[16,48,384]{2,0,1:T(8,128)(2,1)S(1)}, u32[]{:S(2)}, u32[]{:S(2)}) collective-permute-start(bf16[16,48,384]{2,0,1:T(8,128)(2,1)S(1)} %get-tuple-element.107), channel_id=1, source_target_pairs={{0,24},{4,28},{8,16},{12,20},{16,8},{20,12},{24,0},{28,4},{1,25},{... | collective-permute-start | bytes 1769480 | tf_op jit(solution)/shard_map/ppermute | solution.py:349
  313.6 29.3 %collective-permute-start.15 = (bf16[16,48,384]{2,0,1:T(8,128)(2,1)S(1)}, bf16[16,48,384]{2,0,1:T(8,128)(2,1)S(1)}, u32[]{:S(2)}, u32[]{:S(2)}) collective-permute-start(bf16[16,48,384]{2,0,1:T(8,128)(2,1)S(1)} %get-tuple-element.108), channel_id=1, source_target_pairs={{0,16},{4,20},{8,24},{12,28},{16,0},{20,4},{24,8},{28,12},{1,17},{... | collective-permute-start | bytes 1769480 | tf_op jit(solution)/shard_map/ppermute | solution.py:349
  315.5 49.8 %collective-permute-start.17 = (bf16[2,192,768]{2,1,0:T(8,128)(2,1)}, bf16[2,192,768]{2,1,0:T(8,128)(2,1)}, u32[]{:S(2)}, u32[]{:S(2)}) collective-permute-start(bf16[2,192,768]{2,1,0:T(8,128)(2,1)} %get-tuple-element.109), channel_id=1, source_target_pairs={{0,1},{1,0},{2,3},{3,2},{4,5},{5,4},{6,7},{7,6},{8,9},{9,8},{10,11... | collective-permute-start | bytes 1769480 | tf_op jit(solution)/shard_map/ppermute | solution.py:349
  318.3 47.1 %collective-permute-start.19 = (bf16[2,192,768]{2,1,0:T(8,128)(2,1)S(1)}, bf16[2,192,768]{2,1,0:T(8,128)(2,1)}, u32[]{:S(2)}, u32[]{:S(2)}) collective-permute-start(bf16[2,192,768]{2,1,0:T(8,128)(2,1)S(1)} %get-tuple-element.110), channel_id=1, source_target_pairs={{0,3},{1,2},{2,1},{3,0},{4,7},{5,6},{6,5},{7,4},{8,11},{9,10},{10,... | collective-permute-start | bytes 1769480 | tf_op jit(solution)/shard_map/ppermute | solution.py:349
  329.6 46.1 %collective-permute-start.18 = (bf16[2,192,768]{2,1,0:T(8,128)(2,1)S(1)}, bf16[2,192,768]{2,1,0:T(8,128)(2,1)}, u32[]{:S(2)}, u32[]{:S(2)}) collective-permute-start(bf16[2,192,768]{2,1,0:T(8,128)(2,1)S(1)} %get-tuple-element.111), channel_id=1, source_target_pairs={{0,2},{1,3},{2,0},{3,1},{4,6},{5,7},{6,4},{7,5},{8,10},{9,11},{10,... | collective-permute-start | bytes 1769480 | tf_op jit(solution)/shard_map/ppermute | solution.py:349
  344.3 126.7 %reduce-scatter.8.cloned.1.call-start = ((), (), s32[]{:S(2)}) async-start(), calls=%async_computation.5 | async-start | bytes 2027520 | tf_op jit(solution)/shard_map/reduce_scatter | solution.py:639
  365.3 12.3 %copy-start.7 = (f32[2,192,768]{2,1,0:T(8,128)S(1)}, f32[2,192,768]{2,1,0:T(8,128)}, u32[]{:S(2)}) copy-start(f32[2,192,768]{2,1,0:T(8,128)} %constant_dynamic-slice_fusion) | copy-start | bytes 3538948
  365.3 12.3 %copy-start.21 = (bf16[32,24,768]{2,1,0:T(8,128)(2,1)S(1)}, bf16[32,24,768]{2,1,0:T(8,128)(2,1)}, u32[]{:S(2)}) copy-start(bf16[32,24,768]{2,1,0:T(8,128)(2,1)} %copy-done.20) | copy-start | bytes 3538948
  365.3 12.3 %copy-start.23 = (bf16[32,24,768]{2,1,0:T(8,128)(2,1)S(1)}, bf16[32,24,768]{2,1,0:T(8,128)(2,1)}, u32[]{:S(2)}) copy-start(bf16[32,24,768]{2,1,0:T(8,128)(2,1)} %copy-done.22) | copy-start | bytes 3538948
  389.2 4.5 collective-permute-start.20
  395.5 18.7 %collective-permute-start.21 = (bf16[368,768]{1,0:T(8,128)(2,1)}, bf16[368,768]{1,0:T(8,128)(2,1)}, u32[]{:S(2)}, u32[]{:S(2)}) collective-permute-start(bf16[368,768]{1,0:T(8,128)(2,1)} %get-tuple-element.112), channel_id=1, source_target_pairs={{0,8},{4,12},{8,0},{12,4},{16,24},{20,28},{24,16},{28,20},{1,9},{5... | collective-permute-start | bytes 1695752 | tf_op jit(solution)/shard_map/ppermute | solution.py:349
  397.0 30.0 %collective-permute-start.23 = (bf16[368,768]{1,0:T(8,128)(2,1)}, bf16[368,768]{1,0:T(8,128)(2,1)}, u32[]{:S(2)}, u32[]{:S(2)}) collective-permute-start(bf16[368,768]{1,0:T(8,128)(2,1)} %get-tuple-element.113), channel_id=1, source_target_pairs={{0,24},{4,28},{8,16},{12,20},{16,8},{20,12},{24,0},{28,4},{1,25},{... | collective-permute-start | bytes 1695752 | tf_op jit(solution)/shard_map/ppermute | solution.py:349
  398.3 28.7 %collective-permute-start.22 = (bf16[368,768]{1,0:T(8,128)(2,1)}, bf16[368,768]{1,0:T(8,128)(2,1)}, u32[]{:S(2)}, u32[]{:S(2)}) collective-permute-start(bf16[368,768]{1,0:T(8,128)(2,1)} %get-tuple-element.114), channel_id=1, source_target_pairs={{0,16},{4,20},{8,24},{12,28},{16,0},{20,4},{24,8},{28,12},{1,17},{... | collective-permute-start | bytes 1695752 | tf_op jit(solution)/shard_map/ppermute | solution.py:349
  408.7 21.2 %collective-permute-start.24 = (f32[32,512]{1,0:T(8,128)S(1)}, f32[32,512]{1,0:T(8,128)S(1)}, u32[]{:S(2)}, u32[]{:S(2)}) collective-permute-start(f32[32,512]{1,0:T(8,128)S(1)} %select_maximum_fusion), channel_id=1, source_target_pairs={{0,1},{1,0},{2,3},{3,2},{4,5},{5,4},{6,7},{7,6},{8,9},{9,8},{10,11... | collective-permute-start | bytes 196616 | tf_op jit(solution)/shard_map/ppermute | solution.py:349
  429.9 10.3 %collective-permute-start.25 = (f32[32,512]{1,0:T(8,128)S(1)}, f32[32,512]{1,0:T(8,128)S(1)}, u32[]{:S(2)}, u32[]{:S(2)}) collective-permute-start(f32[32,512]{1,0:T(8,128)S(1)} %add_add_fusion), channel_id=1, source_target_pairs={{0,2},{1,3},{2,0},{3,1},{4,6},{5,7},{6,4},{7,5},{8,10},{9,11},{10,... | collective-permute-start | bytes 196616 | tf_op jit(solution)/shard_map/ppermute | solution.py:349
  432.4 14.2 %collective-permute-start.29 = (bf16[80,768]{1,0:T(8,128)(2,1)S(1)}, bf16[80,768]{1,0:T(8,128)(2,1)S(1)}, u32[]{:S(2)}, u32[]{:S(2)}) collective-permute-start(bf16[80,768]{1,0:T(8,128)(2,1)S(1)} %get-tuple-element.119), channel_id=1, source_target_pairs={{0,1},{1,0},{2,3},{3,2},{4,5},{5,4},{6,7},{7,6},{8,9},{9,8},{10,11... | collective-permute-start | bytes 368648 | tf_op jit(solution)/shard_map/ppermute | solution.py:349
  434.0 14.7 %collective-permute-start.31 = (bf16[80,768]{1,0:T(8,128)(2,1)S(1)}, bf16[80,768]{1,0:T(8,128)(2,1)S(1)}, u32[]{:S(2)}, u32[]{:S(2)}) collective-permute-start(bf16[80,768]{1,0:T(8,128)(2,1)S(1)} %get-tuple-element.120), channel_id=1, source_target_pairs={{0,3},{1,2},{2,1},{3,0},{4,7},{5,6},{6,5},{7,4},{8,11},{9,10},{10,... | collective-permute-start | bytes 368648 | tf_op jit(solution)/shard_map/ppermute | solution.py:349
  434.5 24.8 %collective-permute-start.30 = (bf16[80,768]{1,0:T(8,128)(2,1)S(1)}, bf16[80,768]{1,0:T(8,128)(2,1)S(1)}, u32[]{:S(2)}, u32[]{:S(2)}) collective-permute-start(bf16[80,768]{1,0:T(8,128)(2,1)S(1)} %get-tuple-element.121), channel_id=1, source_target_pairs={{0,2},{1,3},{2,0},{3,1},{4,6},{5,7},{6,4},{7,5},{8,10},{9,11},{10,... | collective-permute-start | bytes 368648 | tf_op jit(solution)/shard_map/ppermute | solution.py:349
  440.3 20.3 %collective-permute-start.26 = (f32[32,512]{1,0:T(8,128)S(1)}, f32[32,512]{1,0:T(8,128)S(1)}, u32[]{:S(2)}, u32[]{:S(2)}) collective-permute-start(f32[32,512]{1,0:T(8,128)S(1)} %add.456), channel_id=1, source_target_pairs={{0,4},{4,0},{8,12},{12,8},{16,20},{20,16},{24,28},{28,24},{1,5},{5... | collective-permute-start | bytes 196616 | tf_op jit(solution)/shard_map/ppermute | solution.py:349
  460.5 4.3 collective-permute-start.27
  464.9 4.3 collective-permute-start.28
  (46 other events, 98.2 us)
Sparse Core Ops, SparseCore 0:
  13.7 108.1 all-gather.7
  133.4 56.8 all-gather.5
  243.2 80.0 reduce-scatter.3
  344.4 61.7 reduce-scatter.5
  408.7 47.6 reduce-scatter.7
